TPU v7x, 512 devices: a whole 4x4x16 slice. The times are simulated.
512 devices in a mesh: row: 16 (over x, z_lo), col: 32 (over z_hi, y, core).
Axes of the slice: x: 4, y: 4, z: 16 (z_hi: 4, z_lo: 4; z = z_hi * 4 + z_lo), core: 2. Of those that a mesh axis runs over, the one named last changes fastest.
Arguments:
- grad_out: bfloat16 [2048, 8192], P('col', 'row'), may hold values from -6 to 6
- gate_act: bfloat16 [2048, 28672], P('row', 'col'), may hold values from -6 to 6
- up_act: bfloat16 [2048, 28672], P('row', 'col'), may hold values from -6 to 6
- down_weight: bfloat16 [28672, 8192], P('col', 'row'), may hold values from -0.0625 to 0.0625
- counts: int32 [16], P('row'), may hold values from 32 to 128, as said below
- down_seed: int32 [1], replicated, may hold values from 0 to 1073741823
- up_seed: int32 [1], replicated, may hold values from 0 to 1073741823
Outputs:
- gate_grad: bfloat16 [2048, 28672], P('row', 'col')
- up_grad: bfloat16 [2048, 28672], P('row', 'col')
- features: float32 [16, 64, 64], P('row', 'col')
Inputs may be any that keep to these rules, and one draw needn't show every extreme that they name: counts[e] is how many leading positions of example e carry tokens; some example has all 128 positions in every draw.
All inputs are finite; a program needn't handle non-finite values.
Results may differ from a plain program's by a relative error of at most 0.0027.
Values may be sent and summed in bfloat16 or wider, within the bound.
A program may use at most 64 MiB of HBM per device.

v0:
```python
import math

import jax
import jax.numpy as jnp
from jax import lax
from jax.sharding import PartitionSpec as P

D = 8192
FF = 28672
RANK = 64


def scramble(values):
    values = values ^ values >> 16 & 65535
    values = values * 73244475
    values = values ^ values >> 16 & 65535
    values = values * 73244475
    return values ^ values >> 16 & 65535


def projection(seed_value, first_row, row_count, rank_size):
    row_number = first_row + lax.broadcasted_iota(jnp.int32, (row_count, rank_size), 0)
    rank_number = lax.broadcasted_iota(jnp.int32, (row_count, rank_size), 1)
    seed_mix = scramble(seed_value + 40503)
    hashed = scramble(row_number * rank_size + rank_number ^ seed_mix)
    return ((hashed >> 8 & 255).astype(jnp.float32) - 127.5).astype(jnp.bfloat16)


def shards(grad_out, gate_act, up_act, down_weight, counts, down_seed, up_seed):
    row_index = lax.axis_index("row")
    col_index = lax.axis_index("col")
    col_count = lax.axis_size("col")
    block_width = down_weight.shape[1]
    ff_width = down_weight.shape[0]
    tok_rows = gate_act.shape[0]
    up_proj = projection(up_seed, row_index * block_width, block_width, RANK)
    gathered = lax.all_gather(grad_out, "col", axis=0, tiled=True)
    piece_rows = gathered
    hidden_grad = lax.psum_scatter(
        lax.dot_general(
            piece_rows, down_weight, (((1,), (1,)), ((), ())), preferred_element_type=jnp.float32
        ),
        "row",
        scatter_dimension=0,
        tiled=True,
    )
    piece_rows = gathered
    rank_sum = lax.psum_scatter(
        jnp.dot(piece_rows, up_proj, preferred_element_type=jnp.float32),
        "row",
        scatter_dimension=0,
        tiled=True,
    )
    gate_value = gate_act.astype(jnp.float32)
    up_value = up_act.astype(jnp.float32)
    sigmoid_gate = jax.nn.sigmoid(gate_value)
    silu_gate = gate_value * sigmoid_gate
    gate_grad = (
        hidden_grad * up_value * sigmoid_gate * (1.0 + gate_value * (1.0 - sigmoid_gate))
    ).astype(jnp.bfloat16)
    up_grad = (hidden_grad * silu_gate).astype(jnp.bfloat16)
    hidden = (silu_gate * up_value).astype(jnp.bfloat16)
    grad_ranks = rank_sum * (1.0 / math.sqrt(D * 5461.25))
    scale_in = 1.0 / math.sqrt(FF * 5461.25)
    live_count = counts[0]
    owner_share = tok_rows // col_count
    down_proj = projection(down_seed, 0, FF, RANK)
    blocks = hidden.reshape(col_count, owner_share, ff_width)
    owned_ranks = (
        jnp.dot(
            lax.all_to_all(blocks, "col", split_axis=0, concat_axis=2, tiled=True)[0],
            down_proj,
            preferred_element_type=jnp.float32,
        )[None]
        * scale_in
    )[0]
    first_owned = col_index * owner_share
    owned_grads = lax.dynamic_slice_in_dim(grad_ranks, first_owned, owner_share, 0)
    positions = first_owned + lax.broadcasted_iota(jnp.int32, (owner_share, 1), 0)
    masked = owned_ranks * jnp.where(positions < live_count, 1.0, 0.0)
    partial_value = lax.dot_general(
        masked,
        owned_grads,
        (((0,), (0,)), ((), ())),
        precision=lax.Precision.HIGHEST,
        preferred_element_type=jnp.float32,
    )
    features = lax.psum_scatter(partial_value, "col", scatter_dimension=0, tiled=True)
    features = features * lax.rsqrt(live_count.astype(jnp.float32))
    return (gate_grad, up_grad, features[None])


def solution(mesh):
    in_specs = (
        P("col", "row"),
        P("row", "col"),
        P("row", "col"),
        P("col", "row"),
        P("row"),
        P(),
        P(),
    )
    out_specs = (P("row", "col"), P("row", "col"), P("row", "col", None))
    return jax.shard_map(shards, mesh=mesh, in_specs=in_specs, out_specs=out_specs, check_vma=False)
```

profile of v0, /device:TPU:1, one launch (start us, length us, event | category | flops | bytes accessed | tf_op | source)
XLA Modules:
  0.0 542.7 jit_solution(11567191527424566560)
XLA Ops:
  7.2 0.0 copy-start
  7.2 0.0 all-gather.2.cloned.1.call-start
  7.2 0.7 all-gather.2.cloned.1.call-update
  7.9 0.0 copy-start.2
  7.9 0.0 reduce-scatter.3.cloned.1.call-start
  8.0 87.2 %all-gather.2.cloned.1.call-done = bf16[2048,512]{1,0:T(8,128)(2,1)} async-done(((bf16[64,512]{1,0:T(8,128)(2,1)}), bf16[2048,512]{1,0:T(8,128)(2,1)}) %all-gather.2.cloned.1.call-update) | async-done | bytes 2097168 | tf_op jit(solution)/shard_map/all_gather | solution.py:37
  95.2 0.0 copy-done
  95.2 6.9 %fusion.36 = f32[2048,896]{1,0:T(8,128)} fusion(bf16[2048,512]{1,0:T(8,128)(2,1)} %all-gather.2.cloned.1.call-done, bf16[896,512]{1,0:T(8,128)(2,1)S(1)} %copy-done), kind=kOutput, calls=%fused_computation.50 | convolution fusion | flops 1879048192 | bytes 10354688 | tf_op jit(solution)/shard_map/dot_general | solution.py:40
  102.1 0.0 reduce-scatter.3.cloned.1.call-update
  102.1 164.3 %reduce-scatter.3.cloned.1.call-done = f32[128,896]{1,0:T(8,128)} async-done(((f32[2048,896]{1,0:T(8,128)}), f32[128,896]{1,0:T(8,128)}) %reduce-scatter.3.cloned.1.call-update) | async-done | bytes 458768 | tf_op jit(solution)/shard_map/reduce_scatter | solution.py:39
  266.5 2.1 multiply_convert_fusion
  268.6 0.7 reshape.23
  269.3 12.9 %all-to-all-start = ((bf16[32,4,896]{2,1,0:T(4,128)(2,1)}), bf16[32,4,896]{2,1,0:T(4,128)(2,1)S(1)}, u32[]{:S(2)}, u32[]{:S(2)}) async-start(bf16[32,4,896]{2,1,0:T(4,128)(2,1)} %reshape.23), calls=%async_computation.1 | async-start | bytes 458752 | tf_op jit(solution)/shard_map/all_to_all | solution.py:71
  282.3 0.0 reduce-scatter.5.cloned.1.call-start
  283.0 0.0 copy-done.1
  283.0 1.5 convolution_bitcast_fusion
  284.5 0.0 reduce-scatter.5.cloned.1.call-update
  285.9 1.3 dynamic-slice
  287.9 14.0 %all-to-all-done = bf16[32,4,896]{2,1,0:T(4,128)(2,1)S(1)} async-done(((bf16[32,4,896]{2,1,0:T(4,128)(2,1)}), bf16[32,4,896]{2,1,0:T(4,128)(2,1)S(1)}, u32[]{:S(2)}, u32[]{:S(2)}) %all-to-all-start) | async-done | bytes 229408 | tf_op jit(solution)/shard_map/all_to_all | solution.py:71
  301.9 3.6 fusion.1
  305.5 58.5 %reduce-scatter.5.cloned.1.call-done = f32[128,64]{0,1:T(8,128)} async-done(((f32[2048,64]{0,1:T(8,128)}), f32[128,64]{0,1:T(8,128)}) %reduce-scatter.5.cloned.1.call-update) | async-done | bytes 32784 | tf_op jit(solution)/shard_map/reduce_scatter | solution.py:48
  364.0 1.0 fusion.18
  365.0 170.6 %all-reduce = f32[64,64]{1,0:T(8,128)S(1)} all-reduce(f32[64,64]{1,0:T(8,128)S(1)} %fusion.18), channel_id=4, replica_groups=mesh['row'=16,'col'=32] {'col'}, use_global_device_ids=true, to_apply=%region_2.3.clone | all-reduce | flops 4096 | bytes 32768
  535.6 0.6 fusion.20
  (5 shorter events, 0.0 us)
Async XLA Ops:
  7.2 88.0 %copy-start = (bf16[896,512]{1,0:T(8,128)(2,1)S(1)}, bf16[896,512]{1,0:T(8,128)(2,1)}, u32[]{:S(2)}) copy-start(bf16[896,512]{1,0:T(8,128)(2,1)} %param.10) | copy-start | bytes 2752516
  7.2 88.0 %all-gather.2.cloned.1.call-start = ((), (), s32[]{:S(2)}) async-start(), calls=%async_computation.3 | async-start | bytes 2162688 | tf_op jit(solution)/shard_map/all_gather | solution.py:37
  7.9 258.6 %copy-start.2 = (bf16[128,896]{1,0:T(8,128)(2,1)S(1)}, bf16[128,896]{1,0:T(8,128)(2,1)}, u32[]{:S(2)}) copy-start(bf16[128,896]{1,0:T(8,128)(2,1)} %param.8) | copy-start | bytes 688132
  7.9 258.6 %reduce-scatter.3.cloned.1.call-start = ((), (), s32[]{:S(2)}) async-start(), calls=%async_computation.4 | async-start | bytes 7798784 | tf_op jit(solution)/shard_map/reduce_scatter | solution.py:39
  102.1 180.9 %copy-start.1 = (bf16[2048,512]{1,0:T(8,128)(2,1)S(1)}, bf16[2048,512]{1,0:T(8,128)(2,1)}, u32[]{:S(2)}) copy-start(bf16[2048,512]{1,0:T(8,128)(2,1)} %all-gather.2.cloned.1.call-done) | copy-start | bytes 6291460
  269.3 32.5 %all-to-all-start = ((bf16[32,4,896]{2,1,0:T(4,128)(2,1)}), bf16[32,4,896]{2,1,0:T(4,128)(2,1)S(1)}, u32[]{:S(2)}, u32[]{:S(2)}) async-start(bf16[32,4,896]{2,1,0:T(4,128)(2,1)} %reshape.23), calls=%async_computation.1 | async-start | bytes 458752 | tf_op jit(solution)/shard_map/all_to_all | solution.py:71
  282.3 81.7 %reduce-scatter.5.cloned.1.call-start = ((), (), s32[]{:S(2)}) async-start(), calls=%async_computation.5 | async-start | bytes 557056 | tf_op jit(solution)/shard_map/reduce_scatter | solution.py:48
Sparse Core Ops, SparseCore 0:
  11.1 83.9 all-gather.1
  102.3 164.1 reduce-scatter.2
  285.9 78.0 reduce-scatter.4
where the time goes:
time: 548 us; the launch traced here: 543 us
  waiting for transfers between devices  325 us (59%)
  blocking collectives  171 us (31%)
  between operations  16.4 us (3%)
  matrix products  13.1 us (2%)
  starting transfers between devices  13 us (2%)
    unnamed x1, blocking collectives  171 us
    reduce_scatter x1, waiting for transfers between devices, shards(): lax.psum_scatter(lax.dot_general(piece_rows, down_weight, (((1,), (1,)),...  164 us
    all_gather x1, waiting for transfers between devices, shards(): gathered = lax.all_gather(grad_out, 'col', axis=0, tiled=True)  87.2 us
    reduce_scatter x1, waiting for transfers between devices, shards(): lax.psum_scatter(jnp.dot(piece_rows, up_proj, preferred_element_type=jnp....  58.5 us
    all_to_all x1, waiting for transfers between devices, shards(): lax.all_to_all(blocks, 'col', split_axis=0, concat_axis=2, tiled=True)[0]  14 us
    all_to_all x1, starting transfers between devices, shards(): lax.all_to_all(blocks, 'col', split_axis=0, concat_axis=2, tiled=True)[0]  12.9 us
  transfers between devices with their start and end apart: 4, of which 4 were waited for; matrix products, arithmetic and copies ran while one was open for 1% of the time, Pallas kernels for 0%

commit v1 on v0

v1 whole, which is shorter than its diff:
```python
import math

import jax
import jax.numpy as jnp
from jax import lax
from jax.experimental import pallas as pl
from jax.experimental.pallas import tpu as pltpu
from jax.sharding import PartitionSpec as P

D = 8192
FF = 28672
RANK = 64
TOK = 128
PIECE = 64
WIDTH = 512
HID = 896
CHUNKS = ((0, 2), (2, 2), (4, 2), (6, 1))
NT = (((1,), (1,)), ((), ()))
MESH = pl.DeviceIdType.MESH
COPIES = 96


def scramble(values):
    values = values ^ values >> 16 & 65535
    values = values * 73244475
    values = values ^ values >> 16 & 65535
    values = values * 73244475
    return values ^ values >> 16 & 65535


def projection_t(seed_value, first_row, row_count):
    row_number = first_row + lax.broadcasted_iota(jnp.int32, (RANK, row_count), 1)
    rank_number = lax.broadcasted_iota(jnp.int32, (RANK, row_count), 0)
    seed_mix = scramble(seed_value + 40503)
    hashed = scramble(row_number * RANK + rank_number ^ seed_mix)
    return ((hashed >> 8 & 255).astype(jnp.float32) - 127.5).astype(jnp.bfloat16)


def kernel(
    grad_ref, gate_ref, up_ref, weight_ref, counts_ref, down_seed_ref, up_seed_ref,
    gate_out, up_out, feat_out,
    gate_in, up_in, weights, zblocks, grads, up_proj, down_proj, hidden,
    gate_factor, up_factor, own, partial, part_out, part_in, rank_out, rank_in,
    feat_z, feat_z_in, feat_y, feat_y_in, feat_c, feat_c_in,
    send_sem, recv_sem, local_sem, cross_send, cross_recv,
):
    row = lax.axis_index("row")
    col = lax.axis_index("col")
    x, zl = lax.div(row, 4), lax.rem(row, 4)
    zh, y, c = lax.div(col, 8), lax.rem(lax.div(col, 2), 4), lax.rem(col, 2)

    def turn(value, step):
        return lax.rem(value + step, 4)

    def device(x=x, zl=zl, zh=zh, y=y, c=c):
        return (x * 4 + zl, (zh * 4 + y) * 2 + c)

    sibling = device(c=1 - c)
    started = []

    def send(src, dst, target):
        index = len(started)
        copy = pltpu.make_async_remote_copy(
            src_ref=src, dst_ref=dst, send_sem=send_sem.at[index], recv_sem=recv_sem.at[index],
            device_id=target, device_id_type=MESH,
        )
        copy.start()
        started.append(copy)
        return copy

    locals_ = []
    for number, (src, dst) in enumerate(
        ((weight_ref, weights.at[x]), (gate_ref, gate_in), (up_ref, up_in))
    ):
        copy = pltpu.make_async_copy(src, dst, local_sem.at[number])
        copy.start()
        locals_.append(copy)

    barrier = pltpu.get_barrier_semaphore()
    peers = [sibling]
    for step in (1, 2, 3):
        peers += [
            device(x=turn(x, step)), device(zl=turn(zl, step)),
            device(zh=turn(zh, step)), device(y=turn(y, step)),
        ]
    for peer in peers:
        pl.semaphore_signal(barrier, inc=1, device_id=peer, device_id_type=MESH)
    pl.semaphore_wait(barrier, len(peers))


    def mine(group):
        return pl.ds(pl.multiple_of(group * TOK + c * PIECE, PIECE), PIECE)

    def cross(step, src):
        target = turn(zh, step)
        slot = grads.at[x, mine(y)]
        remote = pltpu.make_async_remote_copy(
            src_ref=src, dst_ref=slot, send_sem=cross_send.at[step], recv_sem=cross_recv.at[x],
            device_id=device(x=target), device_id_type=MESH,
        )
        local = pltpu.make_async_copy(src, slot, local_sem.at[3])

        @pl.when(target != x)
        def _():
            remote.start()

        @pl.when(target == x)
        def _():
            local.start()

        return target, remote

    def send_weight(chunk):
        first, count = CHUNKS[chunk]
        rows = pl.ds(first * 128, count * 128)
        right = send(weight_ref.at[rows], weights.at[x, rows], device(x=turn(x, 1)))
        left = send(weight_ref.at[rows], weights.at[x, rows], device(x=turn(x, 3)))
        return right, left

    def forward_weight(chunk, copies):
        first, count = CHUNKS[chunk]
        right, left = copies
        half = count * 64
        right.wait_recv()
        rows = pl.ds(first * 128, half)
        block = weights.at[turn(x, 3), rows]
        on_right = send(block, block, device(x=turn(x, 1)))
        left.wait_recv()
        rows = pl.ds(first * 128 + half, half)
        block = weights.at[turn(x, 1), rows]
        on_left = send(block, block, device(x=turn(x, 3)))
        return on_right, on_left

    z_up = send(grad_ref, zblocks.at[zh], device(zh=turn(zh, 1)))
    z_down = send(grad_ref, zblocks.at[zh], device(zh=turn(zh, 3)))
    crossed = [cross(0, grad_ref)]
    w0 = send_weight(0)
    w1 = send_weight(1)

    down_proj[...] = projection_t(down_seed_ref[0], col * HID, HID)
    for part in range(4):
        up_proj[part] = projection_t(up_seed_ref[0], (part * 4 + zl) * WIDTH, WIDTH)
    locals_[1].wait()
    locals_[2].wait()
    for part in range(7):
        cols = slice(part * 128, part * 128 + 128)
        gate_value = gate_in[:, cols].astype(jnp.float32)
        up_value = up_in[:, cols].astype(jnp.float32)
        sigmoid_gate = jax.nn.sigmoid(gate_value)
        silu_gate = gate_value * sigmoid_gate
        gate_factor[:, cols] = up_value * sigmoid_gate * (1.0 + gate_value * (1.0 - sigmoid_gate))
        up_factor[:, cols] = silu_gate
        hidden[:, cols] = (silu_gate * up_value).astype(jnp.bfloat16)

    z_up.wait_recv()
    block = zblocks.at[turn(zh, 3), pl.ds(0, 32)]
    z_on_up = send(block, block, device(zh=turn(zh, 1)))
    crossed.append(cross(3, zblocks.at[turn(zh, 3)]))
    z_down.wait_recv()
    block = zblocks.at[turn(zh, 1), pl.ds(32, 32)]
    z_on_down = send(block, block, device(zh=turn(zh, 3)))
    crossed.append(cross(1, zblocks.at[turn(zh, 1)]))

    w0_on = forward_weight(0, w0)
    w2 = send_weight(2)
    hidden_ranks = lax.dot_general(
        down_proj[...], hidden[...], NT, preferred_element_type=jnp.float32
    ) * (1.0 / math.sqrt(FF * 5461.25))

    z_on_up.wait_recv()
    z_on_down.wait_recv()
    crossed.append(cross(2, zblocks.at[turn(zh, 2)]))
    w3 = send_weight(3)

    pltpu.make_async_copy(grad_ref, grads.at[x, mine(y)], local_sem.at[3]).wait()
    for step in (1, 2, 3):
        source = turn(x, step)
        slot = grads.at[source, mine(y)]
        pltpu.make_async_remote_copy(
            src_ref=slot, dst_ref=slot, send_sem=cross_send.at[step], recv_sem=cross_recv.at[source],
            device_id=device(x=source), device_id_type=MESH,
        ).wait_recv()

    def y_block(source, first=0, count=4):
        return grads.at[pl.ds(first, count), mine(source)]

    block = y_block(y)
    y_up = send(block, block, device(y=turn(y, 1)))
    y_down = send(block, block, device(y=turn(y, 3)))
    across = [send(block, block, sibling)]
    w1_on = forward_weight(1, w1)

    y_up.wait_recv()
    block = y_block(turn(y, 3), 0, 2)
    y_on_up = send(block, block, device(y=turn(y, 1)))
    block = y_block(turn(y, 3))
    across.append(send(block, block, sibling))
    y_down.wait_recv()
    block = y_block(turn(y, 1), 2, 2)
    y_on_down = send(block, block, device(y=turn(y, 3)))
    block = y_block(turn(y, 1))
    across.append(send(block, block, sibling))
    w2_on = forward_weight(2, w2)
    w3_on = forward_weight(3, w3)
    y_on_up.wait_recv()
    block = y_block(turn(y, 2), 0, 2)
    across.append(send(block, block, sibling))
    y_on_down.wait_recv()
    block = y_block(turn(y, 2), 2, 2)
    across.append(send(block, block, sibling))
    for copy in across:
        copy.wait_recv()

    rank_copies = []
    rank_own = None
    for step in (1, 2, 3, 0):
        target = turn(zl, step)
        rows = pl.ds(pl.multiple_of(target * TOK, TOK), TOK)
        total = jnp.zeros((RANK, TOK), jnp.float32)
        for part in range(4):
            total += lax.dot_general(
                up_proj[part], grads[part, rows], NT, preferred_element_type=jnp.float32
            )
        if step:
            rank_out[step - 1] = total
            rank_copies.append(send(rank_out.at[step - 1], rank_in.at[step - 1], device(zl=target)))
        else:
            rank_own = total

    def multiply(chunk):
        first, count = CHUNKS[chunk]
        rows = pl.ds(first * 128, count * 128)
        copies = []
        lanes = slice(0, count * 128)
        for part in range(4):
            product = lax.dot_general(
                grads[part], weights[part, rows], NT, preferred_element_type=jnp.float32
            )
            partial[:, lanes] = product if part == 0 else partial[:, lanes] + product
        for step in (2, 3, 1, 0):
            target = turn(zl, step)
            tokens = pl.ds(pl.multiple_of(target * TOK, TOK), TOK)
            if step:
                for lane in range(count):
                    part_out[step - 1, first + lane] = partial[
                        tokens, lane * 128 : lane * 128 + 128
                    ].astype(jnp.bfloat16)
                blocks = pl.ds(first, count)
                copies.append(
                    send(
                        part_out.at[step - 1, blocks], part_in.at[step - 1, blocks],
                        device(zl=target),
                    )
                )
            else:
                own[:, rows] = partial[tokens, lanes]
        return copies

    def finish(chunk, copies):
        first, count = CHUNKS[chunk]
        for copy in copies:
            copy.wait_recv()
        for lane in range(first, first + count):
            cols = slice(lane * 128, lane * 128 + 128)
            total = own[:, cols]
            for source in range(3):
                total += part_in[source, lane].astype(jnp.float32)
            gate_out[:, cols] = (total * gate_factor[:, cols]).astype(jnp.bfloat16)
            up_out[:, cols] = (total * up_factor[:, cols]).astype(jnp.bfloat16)

    locals_[0].wait()
    parts = []
    for chunk, copies in ((0, w0_on), (1, w1_on)):
        for copy in copies:
            copy.wait_recv()
        parts.append(multiply(chunk))

    for copy in rank_copies:
        copy.wait_recv()
    grad_ranks = (rank_own + rank_in[0] + rank_in[1] + rank_in[2]) * (
        1.0 / math.sqrt(D * 5461.25)
    )
    live_count = counts_ref[0]
    positions = lax.broadcasted_iota(jnp.int32, (RANK, TOK), 1)
    masked = hidden_ranks * jnp.where(positions < live_count, 1.0, 0.0)
    features = lax.dot_general(
        masked, grad_ranks, NT, precision=lax.Precision.HIGHEST, preferred_element_type=jnp.float32
    )
    feat_z[...] = jnp.zeros_like(feat_z)
    for owner in range(32):
        feat_z[owner, 0:2, 0:RANK] = features[owner * 2 : owner * 2 + 2, :]
    z_copies = [
        send(
            feat_z.at[pl.ds(turn(zh, step) * 8, 8)], feat_z_in.at[step - 1],
            device(zh=turn(zh, step)),
        )
        for step in (1, 2, 3)
    ]

    for copy in w2_on:
        copy.wait_recv()
    parts.append(multiply(2))

    for copy in z_copies:
        copy.wait_recv()
    feat_y[...] = feat_z[pl.ds(zh * 8, 8)] + feat_z_in[0] + feat_z_in[1] + feat_z_in[2]
    y_copies = [
        send(
            feat_y.at[pl.ds(turn(y, step) * 2, 2)], feat_y_in.at[step - 1],
            device(y=turn(y, step)),
        )
        for step in (1, 2, 3)
    ]

    for copy in w3_on:
        copy.wait_recv()
    parts.append(multiply(3))

    for copy in y_copies:
        copy.wait_recv()
    feat_c[...] = feat_y[pl.ds(y * 2, 2)] + feat_y_in[0] + feat_y_in[1] + feat_y_in[2]
    c_copy = send(feat_c.at[1 - c], feat_c_in, sibling)

    for chunk in (0, 1, 2):
        finish(chunk, parts[chunk])
    c_copy.wait_recv()
    counted = jnp.full((8, 128), live_count, jnp.int32).astype(jnp.float32)
    result = (feat_c[c] + feat_c_in[...]) * lax.rsqrt(counted)
    feat_out[0] = result[0:2, 0:RANK]
    finish(3, parts[3])

    for copy in started:
        copy.wait_send()
    for target, remote in crossed:

        @pl.when(target != x)
        def _(remote=remote):
            remote.wait_send()


def shards(grad_out, gate_act, up_act, down_weight, counts, down_seed, up_seed):
    hbm = pl.BlockSpec(memory_space=pltpu.HBM)
    smem = pl.BlockSpec(memory_space=pltpu.SMEM)
    vmem = pl.BlockSpec(memory_space=pltpu.VMEM)
    bf16, f32 = jnp.bfloat16, jnp.float32
    return pl.pallas_call(
        kernel,
        out_shape=(
            jax.ShapeDtypeStruct((TOK, HID), bf16),
            jax.ShapeDtypeStruct((TOK, HID), bf16),
            jax.ShapeDtypeStruct((1, 2, RANK), f32),
        ),
        in_specs=[hbm, hbm, hbm, hbm, smem, smem, smem],
        out_specs=(vmem, vmem, vmem),
        scratch_shapes=[
            pltpu.VMEM((TOK, HID), bf16),
            pltpu.VMEM((TOK, HID), bf16),
            pltpu.VMEM((4, HID, WIDTH), bf16),
            pltpu.VMEM((4, PIECE, WIDTH), bf16),
            pltpu.VMEM((4, 4 * TOK, WIDTH), bf16),
            pltpu.VMEM((4, RANK, WIDTH), bf16),
            pltpu.VMEM((RANK, HID), bf16),
            pltpu.VMEM((TOK, HID), bf16),
            pltpu.VMEM((TOK, HID), f32),
            pltpu.VMEM((TOK, HID), f32),
            pltpu.VMEM((TOK, HID), f32),
            pltpu.VMEM((4 * TOK, 256), f32),
            pltpu.VMEM((3, 7, TOK, 128), bf16),
            pltpu.VMEM((3, 7, TOK, 128), bf16),
            pltpu.VMEM((3, RANK, TOK), f32),
            pltpu.VMEM((3, RANK, TOK), f32),
            pltpu.VMEM((32, 8, 128), f32),
            pltpu.VMEM((3, 8, 8, 128), f32),
            pltpu.VMEM((8, 8, 128), f32),
            pltpu.VMEM((3, 2, 8, 128), f32),
            pltpu.VMEM((2, 8, 128), f32),
            pltpu.VMEM((8, 128), f32),
            pltpu.SemaphoreType.DMA((COPIES,)),
            pltpu.SemaphoreType.DMA((COPIES,)),
            pltpu.SemaphoreType.DMA((4,)),
            pltpu.SemaphoreType.DMA((4,)),
            pltpu.SemaphoreType.DMA((4,)),
        ],
        compiler_params=pltpu.CompilerParams(
            collective_id=0, has_side_effects=True, vmem_limit_bytes=60 * 1024 * 1024
        ),
    )(grad_out, gate_act, up_act, down_weight, counts, down_seed, up_seed)


def solution(mesh):
    in_specs = (
        P("col", "row"),
        P("row", "col"),
        P("row", "col"),
        P("col", "row"),
        P("row"),
        P(),
        P(),
    )
    out_specs = (P("row", "col"), P("row", "col"), P("row", "col", None))
    return jax.shard_map(shards, mesh=mesh, in_specs=in_specs, out_specs=out_specs, check_vma=False)
```

time: 548 us -> 93.2 us (0.17)
  the two profiles are of different devices: /device:TPU:1 before, /device:TPU:6 now
where the time goes in v1:
time: 93.2 us; the launch traced here: 93.1 us
  Pallas kernels  87.5 us (94%)
  local copies, waits for them, and re-layouts  2.94 us (3%)
  between operations  2.59 us (3%)
    pallas_call x1, Pallas kernels, shards(): pl.pallas_call(kernel, out_shape=(jax.ShapeDtypeStruct((TOK, HID), bf16),...  87.5 us
    unnamed x7, local copies, waits for them, and re-layouts  2.94 us

profile of v1, /device:TPU:6, one launch (start us, length us, event | category | flops | bytes accessed | tf_op | source)
XLA Modules:
  0.0 93.1 jit_solution(2433614896135226156)
XLA Ops:
  2.6 87.5 %shard_map.94 = (bf16[128,896]{1,0:T(8,128)(2,1)}, bf16[128,896]{1,0:T(8,128)(2,1)}, f32[1,2,64]{2,1,0:T(2,128)}) custom-call(bf16[64,512]{1,0:T(8,128)(2,1)} %grad_ref.1, bf16[128,896]{1,0:T(8,128)(2,1)} %gate_ref.1, bf16[128,896]{1,0:T(8,128)(2,1)} %up_ref.1, bf16[896,512]{1,0:T(8,128)(2,1)} %weight_ref.1, s32[1]{0:T(128)S(6)} %copy.13.counts_ref, ...), custom_call_target="tpu_custom_call" | custom-call | tf_op jit(solution)/shard_map/pallas_call | solution.py:346
  90.1 0.0 copy-start
  90.1 1.7 %copy.16 = bf16[128,896]{1,0:T(8,128)(2,1)} copy(bf16[128,896]{1,0:T(8,128)(2,1)} %get-tuple-element.6) | data formatting | bytes 458752
  91.8 0.0 copy-done
  91.8 0.0 copy-start.1
  91.8 0.7 copy.17
  92.5 0.0 copy-done.1
  92.5 0.6 copy.18
Async XLA Ops:
  90.1 1.7 %copy-start = (bf16[128,896]{1,0:T(8,128)(2,1)S(1)}, bf16[128,896]{1,0:T(8,128)(2,1)}, u32[]{:S(2)}) copy-start(bf16[128,896]{1,0:T(8,128)(2,1)} %get-tuple-element.7) | copy-start | bytes 688132
  91.8 0.7 copy-start.1

commit v2 on v1

--- a/solution.py
+++ b/solution.py
@@ -40,9 +40,9 @@
     grad_ref, gate_ref, up_ref, weight_ref, counts_ref, down_seed_ref, up_seed_ref,
     gate_out, up_out, feat_out,
     gate_in, up_in, weights, zblocks, grads, up_proj, down_proj, hidden,
-    gate_factor, up_factor, own, partial, part_out, part_in, rank_out, rank_in,
-    feat_z, feat_z_in, feat_y, feat_y_in, feat_c, feat_c_in,
-    send_sem, recv_sem, local_sem, cross_send, cross_recv,
+    gate_factor, up_factor, own, part_out, part_in, rank_own, rank_out, rank_in,
+    feat_y, feat_y_in, feat_z, feat_z_in, feat_c, feat_c_in,
+    send_sem, recv_sem, local_sem, cross_send, cross_recv, part_send, part_recv,
 ):
     row = lax.axis_index("row")
     col = lax.axis_index("col")
@@ -162,7 +162,6 @@
     crossed.append(cross(1, zblocks.at[turn(zh, 1)]))
 
     w0_on = forward_weight(0, w0)
-    w2 = send_weight(2)
     hidden_ranks = lax.dot_general(
         down_proj[...], hidden[...], NT, preferred_element_type=jnp.float32
     ) * (1.0 / math.sqrt(FF * 5461.25))
@@ -170,7 +169,7 @@
     z_on_up.wait_recv()
     z_on_down.wait_recv()
     crossed.append(cross(2, zblocks.at[turn(zh, 2)]))
-    w3 = send_weight(3)
+    w2 = send_weight(2)
 
     pltpu.make_async_copy(grad_ref, grads.at[x, mine(y)], local_sem.at[3]).wait()
     for step in (1, 2, 3):
@@ -184,11 +183,88 @@
     def y_block(source, first=0, count=4):
         return grads.at[pl.ds(first, count), mine(source)]
 
+    def part_copy(chunk, step):
+        target = turn(y, step)
+        if chunk == 4:
+            src, dst = rank_out.at[step], rank_in.at[zl]
+        else:
+            first, count = CHUNKS[chunk]
+            src, dst = part_out.at[step, pl.ds(first, count)], part_in.at[zl, pl.ds(first, count)]
+        return pltpu.make_async_remote_copy(
+            src_ref=src, dst_ref=dst, send_sem=part_send.at[chunk * 4 + step],
+            recv_sem=part_recv.at[chunk * 4 + zl], device_id=device(zl=target), device_id_type=MESH,
+        )
+
+    def wait_parts(chunk):
+        for step in (1, 2, 3):
+            source = turn(zl, step)
+            if chunk == 4:
+                block = rank_in.at[source]
+            else:
+                first, count = CHUNKS[chunk]
+                block = part_in.at[source, pl.ds(first, count)]
+            pltpu.make_async_remote_copy(
+                src_ref=block, dst_ref=block, send_sem=part_send.at[chunk * 4 + step],
+                recv_sem=part_recv.at[chunk * 4 + source], device_id=device(zl=source),
+                device_id_type=MESH,
+            ).wait_recv()
+
+    def multiply(chunk, step):
+        target = turn(y, step)
+        tokens = pl.ds(pl.multiple_of(target * TOK, TOK), TOK)
+        total = None
+        for part in range(4):
+            if chunk == 4:
+                left, right = up_proj[part], grads[part, tokens]
+            else:
+                first, count = CHUNKS[chunk]
+                rows = pl.ds(first * 128, count * 128)
+                left, right = grads[part, tokens], weights[part, rows]
+            product = lax.dot_general(left, right, NT, preferred_element_type=jnp.float32)
+            total = product if part == 0 else total + product
+
+        @pl.when(target == zl)
+        def _():
+            if chunk == 4:
+                rank_own[...] = total
+            else:
+                own[:, rows] = total
+
+        @pl.when(target != zl)
+        def _():
+            if chunk == 4:
+                rank_out[step] = total
+            else:
+                for lane in range(count):
+                    part_out[step, first + lane] = total[:, lane * 128 : lane * 128 + 128].astype(
+                        jnp.bfloat16
+                    )
+            part_copy(chunk, step).start()
+
+    def finish(chunk):
+        wait_parts(chunk)
+        first, count = CHUNKS[chunk]
+        for lane in range(first, first + count):
+            cols = slice(lane * 128, lane * 128 + 128)
+            total = own[:, cols]
+            for step in (1, 2, 3):
+                total += part_in[turn(zl, step), lane].astype(jnp.float32)
+            gate_out[:, cols] = (total * gate_factor[:, cols]).astype(jnp.bfloat16)
+            up_out[:, cols] = (total * up_factor[:, cols]).astype(jnp.bfloat16)
+
     block = y_block(y)
     y_up = send(block, block, device(y=turn(y, 1)))
     y_down = send(block, block, device(y=turn(y, 3)))
     across = [send(block, block, sibling)]
     w1_on = forward_weight(1, w1)
+    w3 = send_weight(3)
+
+    locals_[0].wait()
+    across[0].wait_recv()
+    multiply(4, 0)
+    for copy in w0_on:
+        copy.wait_recv()
+    multiply(0, 0)
 
     y_up.wait_recv()
     block = y_block(turn(y, 3), 0, 2)
@@ -200,134 +276,95 @@
     y_on_down = send(block, block, device(y=turn(y, 3)))
     block = y_block(turn(y, 1))
     across.append(send(block, block, sibling))
+    for copy in w1_on:
+        copy.wait_recv()
+    multiply(1, 0)
+
+    across[1].wait_recv()
+    multiply(4, 3)
+    multiply(0, 3)
     w2_on = forward_weight(2, w2)
-    w3_on = forward_weight(3, w3)
+    across[2].wait_recv()
+    multiply(4, 1)
+    multiply(0, 1)
     y_on_up.wait_recv()
     block = y_block(turn(y, 2), 0, 2)
     across.append(send(block, block, sibling))
     y_on_down.wait_recv()
     block = y_block(turn(y, 2), 2, 2)
     across.append(send(block, block, sibling))
-    for copy in across:
-        copy.wait_recv()
-
-    rank_copies = []
-    rank_own = None
-    for step in (1, 2, 3, 0):
-        target = turn(zl, step)
-        rows = pl.ds(pl.multiple_of(target * TOK, TOK), TOK)
-        total = jnp.zeros((RANK, TOK), jnp.float32)
-        for part in range(4):
-            total += lax.dot_general(
-                up_proj[part], grads[part, rows], NT, preferred_element_type=jnp.float32
-            )
-        if step:
-            rank_out[step - 1] = total
-            rank_copies.append(send(rank_out.at[step - 1], rank_in.at[step - 1], device(zl=target)))
-        else:
-            rank_own = total
-
-    def multiply(chunk):
-        first, count = CHUNKS[chunk]
-        rows = pl.ds(first * 128, count * 128)
-        copies = []
-        lanes = slice(0, count * 128)
-        for part in range(4):
-            product = lax.dot_general(
-                grads[part], weights[part, rows], NT, preferred_element_type=jnp.float32
-            )
-            partial[:, lanes] = product if part == 0 else partial[:, lanes] + product
-        for step in (2, 3, 1, 0):
-            target = turn(zl, step)
-            tokens = pl.ds(pl.multiple_of(target * TOK, TOK), TOK)
-            if step:
-                for lane in range(count):
-                    part_out[step - 1, first + lane] = partial[
-                        tokens, lane * 128 : lane * 128 + 128
-                    ].astype(jnp.bfloat16)
-                blocks = pl.ds(first, count)
-                copies.append(
-                    send(
-                        part_out.at[step - 1, blocks], part_in.at[step - 1, blocks],
-                        device(zl=target),
-                    )
-                )
-            else:
-                own[:, rows] = partial[tokens, lanes]
-        return copies
-
-    def finish(chunk, copies):
-        first, count = CHUNKS[chunk]
-        for copy in copies:
-            copy.wait_recv()
-        for lane in range(first, first + count):
-            cols = slice(lane * 128, lane * 128 + 128)
-            total = own[:, cols]
-            for source in range(3):
-                total += part_in[source, lane].astype(jnp.float32)
-            gate_out[:, cols] = (total * gate_factor[:, cols]).astype(jnp.bfloat16)
-            up_out[:, cols] = (total * up_factor[:, cols]).astype(jnp.bfloat16)
-
-    locals_[0].wait()
-    parts = []
-    for chunk, copies in ((0, w0_on), (1, w1_on)):
-        for copy in copies:
-            copy.wait_recv()
-        parts.append(multiply(chunk))
-
-    for copy in rank_copies:
-        copy.wait_recv()
-    grad_ranks = (rank_own + rank_in[0] + rank_in[1] + rank_in[2]) * (
-        1.0 / math.sqrt(D * 5461.25)
-    )
+    multiply(1, 3)
+    multiply(1, 1)
+    w3_on = forward_weight(3, w3)
+
+    across[3].wait_recv()
+    across[4].wait_recv()
+    multiply(4, 2)
+    multiply(0, 2)
+    multiply(1, 2)
+    for copy in w2_on:
+        copy.wait_recv()
+    for step in (0, 3, 1, 2):
+        multiply(2, step)
+
+    wait_parts(4)
+    grad_ranks = rank_own[...]
+    for step in (1, 2, 3):
+        grad_ranks += rank_in[turn(zl, step)]
+    grad_ranks *= 1.0 / math.sqrt(D * 5461.25)
     live_count = counts_ref[0]
     positions = lax.broadcasted_iota(jnp.int32, (RANK, TOK), 1)
     masked = hidden_ranks * jnp.where(positions < live_count, 1.0, 0.0)
     features = lax.dot_general(
         masked, grad_ranks, NT, precision=lax.Precision.HIGHEST, preferred_element_type=jnp.float32
     )
-    feat_z[...] = jnp.zeros_like(feat_z)
+    feat_y[...] = jnp.zeros_like(feat_y)
     for owner in range(32):
-        feat_z[owner, 0:2, 0:RANK] = features[owner * 2 : owner * 2 + 2, :]
+        slot = owner // 2 % 4 * 8 + owner // 8 * 2 + owner % 2
+        feat_y[slot, 0:2, 0:RANK] = features[owner * 2 : owner * 2 + 2, :]
+    y_copies = [
+        send(
+            feat_y.at[pl.ds(turn(y, step) * 8, 8)], feat_y_in.at[step - 1],
+            device(y=turn(y, step)),
+        )
+        for step in (1, 2, 3)
+    ]
+
+    for copy in w3_on:
+        copy.wait_recv()
+    for step in (0, 3, 1, 2):
+        multiply(3, step)
+
+    for copy in y_copies:
+        copy.wait_recv()
+    feat_z[...] = feat_y[pl.ds(y * 8, 8)] + feat_y_in[0] + feat_y_in[1] + feat_y_in[2]
     z_copies = [
         send(
-            feat_z.at[pl.ds(turn(zh, step) * 8, 8)], feat_z_in.at[step - 1],
+            feat_z.at[pl.ds(turn(zh, step) * 2, 2)], feat_z_in.at[step - 1],
             device(zh=turn(zh, step)),
         )
         for step in (1, 2, 3)
     ]
 
-    for copy in w2_on:
-        copy.wait_recv()
-    parts.append(multiply(2))
-
+    finish(0)
+    finish(1)
     for copy in z_copies:
         copy.wait_recv()
-    feat_y[...] = feat_z[pl.ds(zh * 8, 8)] + feat_z_in[0] + feat_z_in[1] + feat_z_in[2]
-    y_copies = [
-        send(
-            feat_y.at[pl.ds(turn(y, step) * 2, 2)], feat_y_in.at[step - 1],
-            device(y=turn(y, step)),
-        )
-        for step in (1, 2, 3)
-    ]
-
-    for copy in w3_on:
-        copy.wait_recv()
-    parts.append(multiply(3))
-
-    for copy in y_copies:
-        copy.wait_recv()
-    feat_c[...] = feat_y[pl.ds(y * 2, 2)] + feat_y_in[0] + feat_y_in[1] + feat_y_in[2]
+    feat_c[...] = feat_z[pl.ds(zh * 2, 2)] + feat_z_in[0] + feat_z_in[1] + feat_z_in[2]
     c_copy = send(feat_c.at[1 - c], feat_c_in, sibling)
-
-    for chunk in (0, 1, 2):
-        finish(chunk, parts[chunk])
+    finish(2)
     c_copy.wait_recv()
     counted = jnp.full((8, 128), live_count, jnp.int32).astype(jnp.float32)
     result = (feat_c[c] + feat_c_in[...]) * lax.rsqrt(counted)
     feat_out[0] = result[0:2, 0:RANK]
-    finish(3, parts[3])
+    finish(3)
+
+    for chunk in range(5):
+        for step in range(4):
+
+            @pl.when(turn(y, step) != zl)
+            def _(chunk=chunk, step=step):
+                part_copy(chunk, step).wait_send()
 
     for copy in started:
         copy.wait_send()
@@ -364,11 +401,11 @@
             pltpu.VMEM((TOK, HID), f32),
             pltpu.VMEM((TOK, HID), f32),
             pltpu.VMEM((TOK, HID), f32),
-            pltpu.VMEM((4 * TOK, 256), f32),
-            pltpu.VMEM((3, 7, TOK, 128), bf16),
-            pltpu.VMEM((3, 7, TOK, 128), bf16),
-            pltpu.VMEM((3, RANK, TOK), f32),
-            pltpu.VMEM((3, RANK, TOK), f32),
+            pltpu.VMEM((4, 7, TOK, 128), bf16),
+            pltpu.VMEM((4, 7, TOK, 128), bf16),
+            pltpu.VMEM((RANK, TOK), f32),
+            pltpu.VMEM((4, RANK, TOK), f32),
+            pltpu.VMEM((4, RANK, TOK), f32),
             pltpu.VMEM((32, 8, 128), f32),
             pltpu.VMEM((3, 8, 8, 128), f32),
             pltpu.VMEM((8, 8, 128), f32),
@@ -380,6 +417,8 @@
             pltpu.SemaphoreType.DMA((4,)),
             pltpu.SemaphoreType.DMA((4,)),
             pltpu.SemaphoreType.DMA((4,)),
+            pltpu.SemaphoreType.DMA((20,)),
+            pltpu.SemaphoreType.DMA((20,)),
         ],
         compiler_params=pltpu.CompilerParams(
             collective_id=0, has_side_effects=True, vmem_limit_bytes=60 * 1024 * 1024

time: 93.2 us -> 85.7 us (0.920)
  the two profiles are of different devices: /device:TPU:6 before, /device:TPU:1 now
where the time goes in v2:
time: 85.7 us; the launch traced here: 85.5 us
  Pallas kernels  80 us (93%)
  local copies, waits for them, and re-layouts  2.94 us (3%)
  between operations  2.59 us (3%)
    pallas_call x1, Pallas kernels, shards(): pl.pallas_call(kernel, out_shape=(jax.ShapeDtypeStruct((TOK, HID), bf16),...  80 us
    unnamed x7, local copies, waits for them, and re-layouts  2.94 us

profile of v2, /device:TPU:1, one launch (start us, length us, event | category | flops | bytes accessed | tf_op | source)
XLA Modules:
  0.0 85.5 jit_solution(3612644069960567520)
XLA Ops:
  2.6 80.0 %shard_map.94 = (bf16[128,896]{1,0:T(8,128)(2,1)}, bf16[128,896]{1,0:T(8,128)(2,1)}, f32[1,2,64]{2,1,0:T(2,128)}) custom-call(bf16[64,512]{1,0:T(8,128)(2,1)} %grad_ref.1, bf16[128,896]{1,0:T(8,128)(2,1)} %gate_ref.1, bf16[128,896]{1,0:T(8,128)(2,1)} %up_ref.1, bf16[896,512]{1,0:T(8,128)(2,1)} %weight_ref.1, s32[1]{0:T(128)S(6)} %copy.13.counts_ref, ...), custom_call_target="tpu_custom_call" | custom-call | tf_op jit(solution)/shard_map/pallas_call | solution.py:383
  82.6 0.0 copy-start
  82.6 1.7 %copy.16 = bf16[128,896]{1,0:T(8,128)(2,1)} copy(bf16[128,896]{1,0:T(8,128)(2,1)} %get-tuple-element.6) | data formatting | bytes 458752
  84.3 0.0 copy-done
  84.3 0.0 copy-start.1
  84.3 0.7 copy.17
  85.0 0.0 copy-done.1
  85.0 0.6 copy.18
Async XLA Ops:
  82.6 1.7 %copy-start = (bf16[128,896]{1,0:T(8,128)(2,1)S(1)}, bf16[128,896]{1,0:T(8,128)(2,1)}, u32[]{:S(2)}) copy-start(bf16[128,896]{1,0:T(8,128)(2,1)} %get-tuple-element.7) | copy-start | bytes 688132
  84.3 0.7 copy-start.1

commit v3 on v2

--- a/solution.py
+++ b/solution.py
@@ -14,7 +14,8 @@
 PIECE = 64
 WIDTH = 512
 HID = 896
-CHUNKS = ((0, 2), (2, 2), (4, 2), (6, 1))
+CHUNKS = ((0, 2), (2, 2), (4, 1), (5, 1), (6, 1))
+RANKS = len(CHUNKS)
 NT = (((1,), (1,)), ((), ()))
 MESH = pl.DeviceIdType.MESH
 COPIES = 96
@@ -39,7 +40,7 @@
 def kernel(
     grad_ref, gate_ref, up_ref, weight_ref, counts_ref, down_seed_ref, up_seed_ref,
     gate_out, up_out, feat_out,
-    gate_in, up_in, weights, zblocks, grads, up_proj, down_proj, hidden,
+    gate_in, up_in, weight_in, weights, zblocks, grads, up_proj, down_proj, hidden,
     gate_factor, up_factor, own, part_out, part_in, rank_own, rank_out, rank_in,
     feat_y, feat_y_in, feat_z, feat_z_in, feat_c, feat_c_in,
     send_sem, recv_sem, local_sem, cross_send, cross_recv, part_send, part_recv,
@@ -70,7 +71,7 @@
 
     locals_ = []
     for number, (src, dst) in enumerate(
-        ((weight_ref, weights.at[x]), (gate_ref, gate_in), (up_ref, up_in))
+        ((weight_ref, weight_in), (gate_ref, gate_in), (up_ref, up_in))
     ):
         copy = pltpu.make_async_copy(src, dst, local_sem.at[number])
         copy.start()
@@ -85,6 +86,10 @@
         ]
     for peer in peers:
         pl.semaphore_signal(barrier, inc=1, device_id=peer, device_id_type=MESH)
+
+    locals_[0].wait()
+    for piece in range(2):
+        weights[x, piece] = weight_in[piece * 128 : piece * 128 + 128, :].T
     pl.semaphore_wait(barrier, len(peers))
 
 
@@ -110,32 +115,35 @@
 
         return target, remote
 
-    def send_weight(chunk):
-        first, count = CHUNKS[chunk]
-        rows = pl.ds(first * 128, count * 128)
-        right = send(weight_ref.at[rows], weights.at[x, rows], device(x=turn(x, 1)))
-        left = send(weight_ref.at[rows], weights.at[x, rows], device(x=turn(x, 3)))
+    def send_weight(piece):
+        block = weights.at[x, piece]
+        right = send(block, block, device(x=turn(x, 1)))
+        left = send(block, block, device(x=turn(x, 3)))
         return right, left
 
-    def forward_weight(chunk, copies):
-        first, count = CHUNKS[chunk]
+    def forward_weight(piece, copies):
         right, left = copies
-        half = count * 64
         right.wait_recv()
-        rows = pl.ds(first * 128, half)
-        block = weights.at[turn(x, 3), rows]
+        block = weights.at[turn(x, 3), piece, pl.ds(0, WIDTH // 2)]
         on_right = send(block, block, device(x=turn(x, 1)))
         left.wait_recv()
-        rows = pl.ds(first * 128 + half, half)
-        block = weights.at[turn(x, 1), rows]
+        block = weights.at[turn(x, 1), piece, pl.ds(WIDTH // 2, WIDTH // 2)]
         on_left = send(block, block, device(x=turn(x, 3)))
         return on_right, on_left
+
+    def wait_weights(*pieces):
+        for copies in pieces:
+            for copy in copies:
+                copy.wait_recv()
 
     z_up = send(grad_ref, zblocks.at[zh], device(zh=turn(zh, 1)))
     z_down = send(grad_ref, zblocks.at[zh], device(zh=turn(zh, 3)))
     crossed = [cross(0, grad_ref)]
     w0 = send_weight(0)
     w1 = send_weight(1)
+
+    for piece in range(2, 7):
+        weights[x, piece] = weight_in[piece * 128 : piece * 128 + 128, :].T
 
     down_proj[...] = projection_t(down_seed_ref[0], col * HID, HID)
     for part in range(4):
@@ -152,6 +160,7 @@
         up_factor[:, cols] = silu_gate
         hidden[:, cols] = (silu_gate * up_value).astype(jnp.bfloat16)
 
+    w0_on = forward_weight(0, w0)
     z_up.wait_recv()
     block = zblocks.at[turn(zh, 3), pl.ds(0, 32)]
     z_on_up = send(block, block, device(zh=turn(zh, 1)))
@@ -161,7 +170,8 @@
     z_on_down = send(block, block, device(zh=turn(zh, 3)))
     crossed.append(cross(1, zblocks.at[turn(zh, 1)]))
 
-    w0_on = forward_weight(0, w0)
+    w1_on = forward_weight(1, w1)
+    w2 = send_weight(2)
     hidden_ranks = lax.dot_general(
         down_proj[...], hidden[...], NT, preferred_element_type=jnp.float32
     ) * (1.0 / math.sqrt(FF * 5461.25))
@@ -169,7 +179,8 @@
     z_on_up.wait_recv()
     z_on_down.wait_recv()
     crossed.append(cross(2, zblocks.at[turn(zh, 2)]))
-    w2 = send_weight(2)
+    w3 = send_weight(3)
+    w2_on = forward_weight(2, w2)
 
     pltpu.make_async_copy(grad_ref, grads.at[x, mine(y)], local_sem.at[3]).wait()
     for step in (1, 2, 3):
@@ -185,7 +196,7 @@
 
     def part_copy(chunk, step):
         target = turn(y, step)
-        if chunk == 4:
+        if chunk == RANKS:
             src, dst = rank_out.at[step], rank_in.at[zl]
         else:
             first, count = CHUNKS[chunk]
@@ -198,7 +209,7 @@
     def wait_parts(chunk):
         for step in (1, 2, 3):
             source = turn(zl, step)
-            if chunk == 4:
+            if chunk == RANKS:
                 block = rank_in.at[source]
             else:
                 first, count = CHUNKS[chunk]
@@ -214,26 +225,30 @@
         tokens = pl.ds(pl.multiple_of(target * TOK, TOK), TOK)
         total = None
         for part in range(4):
-            if chunk == 4:
-                left, right = up_proj[part], grads[part, tokens]
+            left = grads[part, tokens]
+            if chunk == RANKS:
+                product = lax.dot_general(
+                    left, up_proj[part], NT, preferred_element_type=jnp.float32
+                )
             else:
                 first, count = CHUNKS[chunk]
                 rows = pl.ds(first * 128, count * 128)
-                left, right = grads[part, tokens], weights[part, rows]
-            product = lax.dot_general(left, right, NT, preferred_element_type=jnp.float32)
+                right = [weights[part, first + piece] for piece in range(count)]
+                right = jnp.concatenate(right, axis=1) if count > 1 else right[0]
+                product = jnp.dot(left, right, preferred_element_type=jnp.float32)
             total = product if part == 0 else total + product
 
         @pl.when(target == zl)
         def _():
-            if chunk == 4:
+            if chunk == RANKS:
                 rank_own[...] = total
             else:
                 own[:, rows] = total
 
         @pl.when(target != zl)
         def _():
-            if chunk == 4:
-                rank_out[step] = total
+            if chunk == RANKS:
+                rank_out[step] = total.astype(jnp.bfloat16)
             else:
                 for lane in range(count):
                     part_out[step, first + lane] = total[:, lane * 128 : lane * 128 + 128].astype(
@@ -256,15 +271,14 @@
     y_up = send(block, block, device(y=turn(y, 1)))
     y_down = send(block, block, device(y=turn(y, 3)))
     across = [send(block, block, sibling)]
-    w1_on = forward_weight(1, w1)
-    w3 = send_weight(3)
-
-    locals_[0].wait()
+    w4 = send_weight(4)
+    w3_on = forward_weight(3, w3)
+
     across[0].wait_recv()
-    multiply(4, 0)
-    for copy in w0_on:
-        copy.wait_recv()
+    multiply(RANKS, 0)
+    wait_weights(w0_on, w1_on)
     multiply(0, 0)
+    w5 = send_weight(5)
 
     y_up.wait_recv()
     block = y_block(turn(y, 3), 0, 2)
@@ -276,17 +290,15 @@
     y_on_down = send(block, block, device(y=turn(y, 3)))
     block = y_block(turn(y, 1))
     across.append(send(block, block, sibling))
-    for copy in w1_on:
-        copy.wait_recv()
+    wait_weights(w2_on, w3_on)
     multiply(1, 0)
-
-    across[1].wait_recv()
-    multiply(4, 3)
-    multiply(0, 3)
-    w2_on = forward_weight(2, w2)
-    across[2].wait_recv()
-    multiply(4, 1)
-    multiply(0, 1)
+    w4_on = forward_weight(4, w4)
+    w6 = send_weight(6)
+
+    for place, step in ((1, 3), (2, 1)):
+        across[place].wait_recv()
+        multiply(RANKS, step)
+        multiply(0, step)
     y_on_up.wait_recv()
     block = y_block(turn(y, 2), 0, 2)
     across.append(send(block, block, sibling))
@@ -295,28 +307,28 @@
     across.append(send(block, block, sibling))
     multiply(1, 3)
     multiply(1, 1)
-    w3_on = forward_weight(3, w3)
+    w5_on = forward_weight(5, w5)
 
     across[3].wait_recv()
     across[4].wait_recv()
-    multiply(4, 2)
+    multiply(RANKS, 2)
     multiply(0, 2)
     multiply(1, 2)
-    for copy in w2_on:
-        copy.wait_recv()
+    wait_weights(w4_on)
     for step in (0, 3, 1, 2):
         multiply(2, step)
-
-    wait_parts(4)
+    w6_on = forward_weight(6, w6)
+
+    wait_parts(RANKS)
     grad_ranks = rank_own[...]
     for step in (1, 2, 3):
-        grad_ranks += rank_in[turn(zl, step)]
+        grad_ranks += rank_in[turn(zl, step)].astype(jnp.float32)
     grad_ranks *= 1.0 / math.sqrt(D * 5461.25)
     live_count = counts_ref[0]
     positions = lax.broadcasted_iota(jnp.int32, (RANK, TOK), 1)
     masked = hidden_ranks * jnp.where(positions < live_count, 1.0, 0.0)
-    features = lax.dot_general(
-        masked, grad_ranks, NT, precision=lax.Precision.HIGHEST, preferred_element_type=jnp.float32
+    features = jnp.dot(
+        masked, grad_ranks, precision=lax.Precision.HIGHEST, preferred_element_type=jnp.float32
     )
     feat_y[...] = jnp.zeros_like(feat_y)
     for owner in range(32):
@@ -330,11 +342,9 @@
         for step in (1, 2, 3)
     ]
 
-    for copy in w3_on:
-        copy.wait_recv()
+    wait_weights(w5_on)
     for step in (0, 3, 1, 2):
         multiply(3, step)
-
     for copy in y_copies:
         copy.wait_recv()
     feat_z[...] = feat_y[pl.ds(y * 8, 8)] + feat_y_in[0] + feat_y_in[1] + feat_y_in[2]
@@ -345,8 +355,11 @@
         )
         for step in (1, 2, 3)
     ]
-
     finish(0)
+
+    wait_weights(w6_on)
+    for step in (0, 3, 1, 2):
+        multiply(4, step)
     finish(1)
     for copy in z_copies:
         copy.wait_recv()
@@ -358,8 +371,9 @@
     result = (feat_c[c] + feat_c_in[...]) * lax.rsqrt(counted)
     feat_out[0] = result[0:2, 0:RANK]
     finish(3)
-
-    for chunk in range(5):
+    finish(4)
+
+    for chunk in range(RANKS + 1):
         for step in range(4):
 
             @pl.when(turn(y, step) != zl)
@@ -392,7 +406,8 @@
         scratch_shapes=[
             pltpu.VMEM((TOK, HID), bf16),
             pltpu.VMEM((TOK, HID), bf16),
-            pltpu.VMEM((4, HID, WIDTH), bf16),
+            pltpu.VMEM((HID, WIDTH), bf16),
+            pltpu.VMEM((4, 7, WIDTH, 128), bf16),
             pltpu.VMEM((4, PIECE, WIDTH), bf16),
             pltpu.VMEM((4, 4 * TOK, WIDTH), bf16),
             pltpu.VMEM((4, RANK, WIDTH), bf16),
@@ -403,9 +418,9 @@
             pltpu.VMEM((TOK, HID), f32),
             pltpu.VMEM((4, 7, TOK, 128), bf16),
             pltpu.VMEM((4, 7, TOK, 128), bf16),
-            pltpu.VMEM((RANK, TOK), f32),
-            pltpu.VMEM((4, RANK, TOK), f32),
-            pltpu.VMEM((4, RANK, TOK), f32),
+            pltpu.VMEM((TOK, RANK), f32),
+            pltpu.VMEM((4, TOK, RANK), bf16),
+            pltpu.VMEM((4, TOK, RANK), bf16),
             pltpu.VMEM((32, 8, 128), f32),
             pltpu.VMEM((3, 8, 8, 128), f32),
             pltpu.VMEM((8, 8, 128), f32),
@@ -417,8 +432,8 @@
             pltpu.SemaphoreType.DMA((4,)),
             pltpu.SemaphoreType.DMA((4,)),
             pltpu.SemaphoreType.DMA((4,)),
-            pltpu.SemaphoreType.DMA((20,)),
-            pltpu.SemaphoreType.DMA((20,)),
+            pltpu.SemaphoreType.DMA((4 * RANKS + 4,)),
+            pltpu.SemaphoreType.DMA((4 * RANKS + 4,)),
         ],
         compiler_params=pltpu.CompilerParams(
             collective_id=0, has_side_effects=True, vmem_limit_bytes=60 * 1024 * 1024

time: 85.7 us -> 84.3 us (0.984)
  Pallas kernels: 80 us -> 78.6 us
    pallas_call x1, Pallas kernels: 80 us -> 78.6 us  [shards(): pl.pallas_call(kernel, out_shape=(jax.ShapeDtypeStruct((TOK, HID), bf16),...]
where the time goes in v3:
time: 84.3 us; the launch traced here: 84.1 us
  Pallas kernels  78.6 us (93%)
  local copies, waits for them, and re-layouts  2.94 us (3%)
  between operations  2.59 us (3%)
    pallas_call x1, Pallas kernels, shards(): pl.pallas_call(kernel, out_shape=(jax.ShapeDtypeStruct((TOK, HID), bf16),...  78.6 us
    unnamed x7, local copies, waits for them, and re-layouts  2.94 us

profile of v3, /device:TPU:1, one launch (start us, length us, event | category | flops | bytes accessed | tf_op | source)
XLA Modules:
  0.0 84.1 jit_solution(18163138171602863315)
XLA Ops:
  2.6 78.6 %shard_map.94 = (bf16[128,896]{1,0:T(8,128)(2,1)}, bf16[128,896]{1,0:T(8,128)(2,1)}, f32[1,2,64]{2,1,0:T(2,128)}) custom-call(bf16[64,512]{1,0:T(8,128)(2,1)} %grad_ref.1, bf16[128,896]{1,0:T(8,128)(2,1)} %gate_ref.1, bf16[128,896]{1,0:T(8,128)(2,1)} %up_ref.1, bf16[896,512]{1,0:T(8,128)(2,1)} %weight_ref.1, s32[1]{0:T(128)S(6)} %copy.13.counts_ref, ...), custom_call_target="tpu_custom_call" | custom-call | tf_op jit(solution)/shard_map/pallas_call | solution.py:397
  81.2 0.0 copy-start
  81.2 1.7 %copy.16 = bf16[128,896]{1,0:T(8,128)(2,1)} copy(bf16[128,896]{1,0:T(8,128)(2,1)} %get-tuple-element.6) | data formatting | bytes 458752
  82.9 0.0 copy-done
  82.9 0.0 copy-start.1
  82.9 0.7 copy.17
  83.5 0.0 copy-done.1
  83.5 0.6 copy.18
Async XLA Ops:
  81.2 1.7 %copy-start = (bf16[128,896]{1,0:T(8,128)(2,1)S(1)}, bf16[128,896]{1,0:T(8,128)(2,1)}, u32[]{:S(2)}) copy-start(bf16[128,896]{1,0:T(8,128)(2,1)} %get-tuple-element.7) | copy-start | bytes 688132
  82.9 0.7 copy-start.1

commit v4 on v3

--- a/solution.py
+++ b/solution.py
@@ -41,7 +41,7 @@
     grad_ref, gate_ref, up_ref, weight_ref, counts_ref, down_seed_ref, up_seed_ref,
     gate_out, up_out, feat_out,
     gate_in, up_in, weight_in, weights, zblocks, grads, up_proj, down_proj, hidden,
-    gate_factor, up_factor, own, part_out, part_in, rank_own, rank_out, rank_in,
+    gate_factor, up_factor, own, part_out, part_on, part_in, rank_own, rank_out, rank_on, rank_in,
     feat_y, feat_y_in, feat_z, feat_z_in, feat_c, feat_c_in,
     send_sem, recv_sem, local_sem, cross_send, cross_recv, part_send, part_recv,
 ):
@@ -194,34 +194,49 @@
     def y_block(source, first=0, count=4):
         return grads.at[pl.ds(first, count), mine(source)]
 
-    def part_copy(chunk, step):
-        target = turn(y, step)
+    side, inner = lax.div(zl, 2), lax.rem(zl + lax.div(zl, 2), 2) == 1
+    mate = side * 2 + 1 - lax.rem(zl, 2)
+
+    def is_across(target):
+        return lax.div(target, 2) != side
+
+    def part_copy(chunk, kind, target):
         if chunk == RANKS:
-            src, dst = rank_out.at[step], rank_in.at[zl]
+            at = ()
+        else:
+            at = (pl.ds(*CHUNKS[chunk]),)
+        src = (rank_out if chunk == RANKS else part_out).at[(target,) + at]
+        if kind == 1:
+            slot = lax.rem(target, 2)
+            dst = (rank_on if chunk == RANKS else part_on).at[(slot,) + at]
+            sem = 2 + slot
+        else:
+            slot = 0 if kind == 0 else 1
+            dst = (rank_in if chunk == RANKS else part_in).at[(slot,) + at]
+            sem = slot
+        return pltpu.make_async_remote_copy(
+            src_ref=src, dst_ref=dst, send_sem=part_send.at[chunk * 4 + target],
+            recv_sem=part_recv.at[chunk * 4 + sem],
+            device_id=device(zl=target if kind == 2 else mate), device_id_type=MESH,
+        )
+
+    def wait_parts(chunk):
+        part_copy(chunk, 0, mate).wait_recv()
+        part_copy(chunk, 2, lax.rem(zl + 2, 4)).wait_recv()
+
+    def put(chunk, target, total):
+        if chunk == RANKS:
+            rank_out[target] = total.astype(jnp.bfloat16)
         else:
             first, count = CHUNKS[chunk]
-            src, dst = part_out.at[step, pl.ds(first, count)], part_in.at[zl, pl.ds(first, count)]
-        return pltpu.make_async_remote_copy(
-            src_ref=src, dst_ref=dst, send_sem=part_send.at[chunk * 4 + step],
-            recv_sem=part_recv.at[chunk * 4 + zl], device_id=device(zl=target), device_id_type=MESH,
-        )
-
-    def wait_parts(chunk):
-        for step in (1, 2, 3):
-            source = turn(zl, step)
-            if chunk == RANKS:
-                block = rank_in.at[source]
-            else:
-                first, count = CHUNKS[chunk]
-                block = part_in.at[source, pl.ds(first, count)]
-            pltpu.make_async_remote_copy(
-                src_ref=block, dst_ref=block, send_sem=part_send.at[chunk * 4 + step],
-                recv_sem=part_recv.at[chunk * 4 + source], device_id=device(zl=source),
-                device_id_type=MESH,
-            ).wait_recv()
-
-    def multiply(chunk, step):
-        target = turn(y, step)
+            for lane in range(count):
+                part_out[target, first + lane] = total[:, lane * 128 : lane * 128 + 128].astype(
+                    jnp.bfloat16
+                )
+
+    pending = []
+
+    def multiply(chunk, target):
         tokens = pl.ds(pl.multiple_of(target * TOK, TOK), TOK)
         total = None
         for part in range(4):
@@ -232,38 +247,63 @@
                 )
             else:
                 first, count = CHUNKS[chunk]
-                rows = pl.ds(first * 128, count * 128)
                 right = [weights[part, first + piece] for piece in range(count)]
                 right = jnp.concatenate(right, axis=1) if count > 1 else right[0]
                 product = jnp.dot(left, right, preferred_element_type=jnp.float32)
             total = product if part == 0 else total + product
 
-        @pl.when(target == zl)
+        keep = (target == zl) | (is_across(target) & inner)
+
+        @pl.when(keep)
         def _():
             if chunk == RANKS:
-                rank_own[...] = total
+                rank_own[target] = total
             else:
-                own[:, rows] = total
-
-        @pl.when(target != zl)
+                own[target, :, first * 128 : (first + count) * 128] = total
+
+        @pl.when(target == mate)
         def _():
-            if chunk == RANKS:
-                rank_out[step] = total.astype(jnp.bfloat16)
-            else:
-                for lane in range(count):
-                    part_out[step, first + lane] = total[:, lane * 128 : lane * 128 + 128].astype(
-                        jnp.bfloat16
-                    )
-            part_copy(chunk, step).start()
+            put(chunk, target, total)
+            part_copy(chunk, 0, target).start()
+
+        @pl.when(is_across(target) & jnp.logical_not(inner))
+        def _():
+            put(chunk, target, total)
+            part_copy(chunk, 1, target).start()
+
+        pending.append((chunk, target))
+
+    def relay(most=0):
+        while len(pending) > most:
+            chunk, target = pending.pop(0)
+
+            @pl.when(is_across(target) & inner)
+            def _(chunk=chunk, target=target):
+                part_copy(chunk, 1, target).wait_recv()
+                slot = lax.rem(target, 2)
+                if chunk == RANKS:
+                    put(chunk, target, rank_own[target] + rank_on[slot].astype(jnp.float32))
+                else:
+                    first, count = CHUNKS[chunk]
+                    for lane in range(first, first + count):
+                        part_out[target, lane] = (
+                            own[target, :, lane * 128 : lane * 128 + 128]
+                            + part_on[slot, lane].astype(jnp.float32)
+                        ).astype(jnp.bfloat16)
+                part_copy(chunk, 2, target).start()
+
+    def multiply_all(chunk):
+        for target in (2 - side * 2, 3 - side * 2, mate, zl):
+            multiply(chunk, target)
 
     def finish(chunk):
         wait_parts(chunk)
         first, count = CHUNKS[chunk]
         for lane in range(first, first + count):
             cols = slice(lane * 128, lane * 128 + 128)
-            total = own[:, cols]
-            for step in (1, 2, 3):
-                total += part_in[turn(zl, step), lane].astype(jnp.float32)
+            total = own[zl, :, cols]
+            for source in range(2):
+                total += part_in[source, lane].astype(jnp.float32)
             gate_out[:, cols] = (total * gate_factor[:, cols]).astype(jnp.bfloat16)
             up_out[:, cols] = (total * up_factor[:, cols]).astype(jnp.bfloat16)
 
@@ -275,11 +315,12 @@
     w3_on = forward_weight(3, w3)
 
     across[0].wait_recv()
-    multiply(RANKS, 0)
+    multiply(RANKS, turn(y, 0))
     wait_weights(w0_on, w1_on)
-    multiply(0, 0)
+    multiply(0, turn(y, 0))
     w5 = send_weight(5)
 
+    relay()
     y_up.wait_recv()
     block = y_block(turn(y, 3), 0, 2)
     y_on_up = send(block, block, device(y=turn(y, 1)))
@@ -291,38 +332,42 @@
     block = y_block(turn(y, 1))
     across.append(send(block, block, sibling))
     wait_weights(w2_on, w3_on)
-    multiply(1, 0)
+    multiply(1, turn(y, 0))
+    relay()
     w4_on = forward_weight(4, w4)
     w6 = send_weight(6)
 
     for place, step in ((1, 3), (2, 1)):
         across[place].wait_recv()
-        multiply(RANKS, step)
-        multiply(0, step)
+        multiply(RANKS, turn(y, step))
+        multiply(0, turn(y, step))
+        relay(2)
     y_on_up.wait_recv()
     block = y_block(turn(y, 2), 0, 2)
     across.append(send(block, block, sibling))
     y_on_down.wait_recv()
     block = y_block(turn(y, 2), 2, 2)
     across.append(send(block, block, sibling))
-    multiply(1, 3)
-    multiply(1, 1)
+    multiply(1, turn(y, 3))
+    multiply(1, turn(y, 1))
+    relay()
     w5_on = forward_weight(5, w5)
 
     across[3].wait_recv()
     across[4].wait_recv()
-    multiply(RANKS, 2)
-    multiply(0, 2)
-    multiply(1, 2)
+    multiply(RANKS, turn(y, 2))
+    multiply(0, turn(y, 2))
+    relay(2)
+    multiply(1, turn(y, 2))
     wait_weights(w4_on)
-    for step in (0, 3, 1, 2):
-        multiply(2, step)
+    multiply_all(2)
+    relay()
     w6_on = forward_weight(6, w6)
 
     wait_parts(RANKS)
-    grad_ranks = rank_own[...]
-    for step in (1, 2, 3):
-        grad_ranks += rank_in[turn(zl, step)].astype(jnp.float32)
+    grad_ranks = rank_own[zl]
+    for source in range(2):
+        grad_ranks += rank_in[source].astype(jnp.float32)
     grad_ranks *= 1.0 / math.sqrt(D * 5461.25)
     live_count = counts_ref[0]
     positions = lax.broadcasted_iota(jnp.int32, (RANK, TOK), 1)
@@ -343,8 +388,8 @@
     ]
 
     wait_weights(w5_on)
-    for step in (0, 3, 1, 2):
-        multiply(3, step)
+    multiply_all(3)
+    relay()
     for copy in y_copies:
         copy.wait_recv()
     feat_z[...] = feat_y[pl.ds(y * 8, 8)] + feat_y_in[0] + feat_y_in[1] + feat_y_in[2]
@@ -358,8 +403,8 @@
     finish(0)
 
     wait_weights(w6_on)
-    for step in (0, 3, 1, 2):
-        multiply(4, step)
+    multiply_all(4)
+    relay()
     finish(1)
     for copy in z_copies:
         copy.wait_recv()
@@ -374,11 +419,11 @@
     finish(4)
 
     for chunk in range(RANKS + 1):
-        for step in range(4):
-
-            @pl.when(turn(y, step) != zl)
-            def _(chunk=chunk, step=step):
-                part_copy(chunk, step).wait_send()
+        for target in range(4):
+
+            @pl.when(zl != target)
+            def _(chunk=chunk, target=target):
+                part_copy(chunk, 2, target).wait_send()
 
     for copy in started:
         copy.wait_send()
@@ -415,12 +460,14 @@
             pltpu.VMEM((TOK, HID), bf16),
             pltpu.VMEM((TOK, HID), f32),
             pltpu.VMEM((TOK, HID), f32),
-            pltpu.VMEM((TOK, HID), f32),
+            pltpu.VMEM((4, TOK, HID), f32),
             pltpu.VMEM((4, 7, TOK, 128), bf16),
-            pltpu.VMEM((4, 7, TOK, 128), bf16),
-            pltpu.VMEM((TOK, RANK), f32),
+            pltpu.VMEM((2, 7, TOK, 128), bf16),
+            pltpu.VMEM((2, 7, TOK, 128), bf16),
+            pltpu.VMEM((4, TOK, RANK), f32),
             pltpu.VMEM((4, TOK, RANK), bf16),
-            pltpu.VMEM((4, TOK, RANK), bf16),
+            pltpu.VMEM((2, TOK, RANK), bf16),
+            pltpu.VMEM((2, TOK, RANK), bf16),
             pltpu.VMEM((32, 8, 128), f32),
             pltpu.VMEM((3, 8, 8, 128), f32),
             pltpu.VMEM((8, 8, 128), f32),

time: 84.3 us -> 85.3 us (1.012)
  Pallas kernels: 78.6 us -> 79.6 us
    pallas_call x1, Pallas kernels: 78.6 us -> 79.6 us  [shards(): pl.pallas_call(kernel, out_shape=(jax.ShapeDtypeStruct((TOK, HID), bf16),...]
where the time goes in v4:
time: 85.3 us; the launch traced here: 85.1 us
  Pallas kernels  79.6 us (93%)
  local copies, waits for them, and re-layouts  2.94 us (3%)
  between operations  2.59 us (3%)
    pallas_call x1, Pallas kernels, shards(): pl.pallas_call(kernel, out_shape=(jax.ShapeDtypeStruct((TOK, HID), bf16),...  79.6 us
    unnamed x7, local copies, waits for them, and re-layouts  2.94 us

profile of v4, /device:TPU:1, one launch (start us, length us, event | category | flops | bytes accessed | tf_op | source)
XLA Modules:
  0.0 85.1 jit_solution(10205553833586642345)
XLA Ops:
  2.6 79.6 %shard_map.94 = (bf16[128,896]{1,0:T(8,128)(2,1)}, bf16[128,896]{1,0:T(8,128)(2,1)}, f32[1,2,64]{2,1,0:T(2,128)}) custom-call(bf16[64,512]{1,0:T(8,128)(2,1)} %grad_ref.1, bf16[128,896]{1,0:T(8,128)(2,1)} %gate_ref.1, bf16[128,896]{1,0:T(8,128)(2,1)} %up_ref.1, bf16[896,512]{1,0:T(8,128)(2,1)} %weight_ref.1, s32[1]{0:T(128)S(6)} %copy.13.counts_ref, ...), custom_call_target="tpu_custom_call" | custom-call | tf_op jit(solution)/shard_map/pallas_call | solution.py:442
  82.2 0.0 copy-start
  82.2 1.7 %copy.16 = bf16[128,896]{1,0:T(8,128)(2,1)} copy(bf16[128,896]{1,0:T(8,128)(2,1)} %get-tuple-element.6) | data formatting | bytes 458752
  83.9 0.0 copy-done
  83.9 0.0 copy-start.1
  83.9 0.7 copy.17
  84.6 0.0 copy-done.1
  84.6 0.6 copy.18
Async XLA Ops:
  82.2 1.7 %copy-start = (bf16[128,896]{1,0:T(8,128)(2,1)S(1)}, bf16[128,896]{1,0:T(8,128)(2,1)}, u32[]{:S(2)}) copy-start(bf16[128,896]{1,0:T(8,128)(2,1)} %get-tuple-element.7) | copy-start | bytes 688132
  83.9 0.7 copy-start.1

commit v5 on v3

--- a/solution.py
+++ b/solution.py
@@ -88,8 +88,11 @@
         pl.semaphore_signal(barrier, inc=1, device_id=peer, device_id_type=MESH)
 
     locals_[0].wait()
-    for piece in range(2):
-        weights[x, piece] = weight_in[piece * 128 : piece * 128 + 128, :].T
+    def turn_weight(*pieces):
+        for piece in pieces:
+            weights[x, piece] = weight_in[piece * 128 : piece * 128 + 128, :].T
+
+    turn_weight(0, 1)
     pl.semaphore_wait(barrier, len(peers))
 
 
@@ -142,12 +145,7 @@
     w0 = send_weight(0)
     w1 = send_weight(1)
 
-    for piece in range(2, 7):
-        weights[x, piece] = weight_in[piece * 128 : piece * 128 + 128, :].T
-
-    down_proj[...] = projection_t(down_seed_ref[0], col * HID, HID)
-    for part in range(4):
-        up_proj[part] = projection_t(up_seed_ref[0], (part * 4 + zl) * WIDTH, WIDTH)
+    turn_weight(2)
     locals_[1].wait()
     locals_[2].wait()
     for part in range(7):
@@ -160,7 +158,6 @@
         up_factor[:, cols] = silu_gate
         hidden[:, cols] = (silu_gate * up_value).astype(jnp.bfloat16)
 
-    w0_on = forward_weight(0, w0)
     z_up.wait_recv()
     block = zblocks.at[turn(zh, 3), pl.ds(0, 32)]
     z_on_up = send(block, block, device(zh=turn(zh, 1)))
@@ -170,17 +167,23 @@
     z_on_down = send(block, block, device(zh=turn(zh, 3)))
     crossed.append(cross(1, zblocks.at[turn(zh, 1)]))
 
+    w0_on = forward_weight(0, w0)
     w1_on = forward_weight(1, w1)
     w2 = send_weight(2)
-    hidden_ranks = lax.dot_general(
-        down_proj[...], hidden[...], NT, preferred_element_type=jnp.float32
-    ) * (1.0 / math.sqrt(FF * 5461.25))
+    turn_weight(3, 4)
+    for part in range(4):
+        up_proj[part] = projection_t(up_seed_ref[0], (part * 4 + zl) * WIDTH, WIDTH)
 
     z_on_up.wait_recv()
     z_on_down.wait_recv()
     crossed.append(cross(2, zblocks.at[turn(zh, 2)]))
     w3 = send_weight(3)
     w2_on = forward_weight(2, w2)
+    turn_weight(5, 6)
+    down_proj[...] = projection_t(down_seed_ref[0], col * HID, HID)
+    hidden_ranks = lax.dot_general(
+        down_proj[...], hidden[...], NT, preferred_element_type=jnp.float32
+    ) * (1.0 / math.sqrt(FF * 5461.25))
 
     pltpu.make_async_copy(grad_ref, grads.at[x, mine(y)], local_sem.at[3]).wait()
     for step in (1, 2, 3):
@@ -397,9 +400,9 @@
     return pl.pallas_call(
         kernel,
         out_shape=(
-            jax.ShapeDtypeStruct((TOK, HID), bf16),
-            jax.ShapeDtypeStruct((TOK, HID), bf16),
-            jax.ShapeDtypeStruct((1, 2, RANK), f32),
+            pltpu.VMEM((TOK, HID), bf16),
+            pltpu.VMEM((TOK, HID), bf16),
+            pltpu.VMEM((1, 2, RANK), f32),
         ),
         in_specs=[hbm, hbm, hbm, hbm, smem, smem, smem],
         out_specs=(vmem, vmem, vmem),

time: 84.3 us -> 83 us (0.985)
  local copies, waits for them, and re-layouts: 2.94 us -> 1.94 us
    unnamed x7 -> x3, local copies, waits for them, and re-layouts: 2.94 us -> 1.94 us
where the time goes in v5:
time: 83 us; the launch traced here: 82.9 us
  Pallas kernels  78.3 us (94%)
  between operations  2.58 us (3%)
  local copies, waits for them, and re-layouts  1.94 us (2%)
    pallas_call x1, Pallas kernels, shards(): pl.pallas_call(kernel, out_shape=(pltpu.VMEM((TOK, HID), bf16), pltpu.VME...  78.3 us
    unnamed x3, local copies, waits for them, and re-layouts  1.94 us

profile of v5, /device:TPU:1, one launch (start us, length us, event | category | flops | bytes accessed | tf_op | source)
XLA Modules:
  0.0 82.9 jit_solution(15554620540077318693)
XLA Ops:
  2.6 78.3 %shard_map.94 = (bf16[128,896]{1,0:T(8,128)(2,1)S(1)}, bf16[128,896]{1,0:T(8,128)(2,1)S(1)}, f32[1,2,64]{2,1,0:T(2,128)S(1)}) custom-call(bf16[64,512]{1,0:T(8,128)(2,1)} %grad_ref.1, bf16[128,896]{1,0:T(8,128)(2,1)} %gate_ref.1, bf16[128,896]{1,0:T(8,128)(2,1)} %up_ref.1, bf16[896,512]{1,0:T(8,128)(2,1)} %weight_ref.1, s32[1]{0:T(128)S(6)} %copy.16.counts_ref, ...), custom_call_target="tpu_custom_call" | custom-call | tf_op jit(solution)/shard_map/pallas_call | solution.py:400
  80.9 0.7 copy.13
  81.6 0.6 copy.15
  82.2 0.7 copy.14

commit v6 on v4

--- a/solution.py
+++ b/solution.py
@@ -15,6 +15,7 @@
 WIDTH = 512
 HID = 896
 CHUNKS = ((0, 2), (2, 2), (4, 1), (5, 1), (6, 1))
+DIRECT = (3, 4)
 RANKS = len(CHUNKS)
 NT = (((1,), (1,)), ((), ()))
 MESH = pl.DeviceIdType.MESH
@@ -88,8 +89,11 @@
         pl.semaphore_signal(barrier, inc=1, device_id=peer, device_id_type=MESH)
 
     locals_[0].wait()
-    for piece in range(2):
-        weights[x, piece] = weight_in[piece * 128 : piece * 128 + 128, :].T
+    def turn_weight(*pieces):
+        for piece in pieces:
+            weights[x, piece] = weight_in[piece * 128 : piece * 128 + 128, :].T
+
+    turn_weight(0, 1)
     pl.semaphore_wait(barrier, len(peers))
 
 
@@ -142,12 +146,7 @@
     w0 = send_weight(0)
     w1 = send_weight(1)
 
-    for piece in range(2, 7):
-        weights[x, piece] = weight_in[piece * 128 : piece * 128 + 128, :].T
-
-    down_proj[...] = projection_t(down_seed_ref[0], col * HID, HID)
-    for part in range(4):
-        up_proj[part] = projection_t(up_seed_ref[0], (part * 4 + zl) * WIDTH, WIDTH)
+    turn_weight(2)
     locals_[1].wait()
     locals_[2].wait()
     for part in range(7):
@@ -160,7 +159,6 @@
         up_factor[:, cols] = silu_gate
         hidden[:, cols] = (silu_gate * up_value).astype(jnp.bfloat16)
 
-    w0_on = forward_weight(0, w0)
     z_up.wait_recv()
     block = zblocks.at[turn(zh, 3), pl.ds(0, 32)]
     z_on_up = send(block, block, device(zh=turn(zh, 1)))
@@ -170,17 +168,23 @@
     z_on_down = send(block, block, device(zh=turn(zh, 3)))
     crossed.append(cross(1, zblocks.at[turn(zh, 1)]))
 
+    w0_on = forward_weight(0, w0)
     w1_on = forward_weight(1, w1)
     w2 = send_weight(2)
-    hidden_ranks = lax.dot_general(
-        down_proj[...], hidden[...], NT, preferred_element_type=jnp.float32
-    ) * (1.0 / math.sqrt(FF * 5461.25))
+    turn_weight(3, 4)
+    for part in range(4):
+        up_proj[part] = projection_t(up_seed_ref[0], (part * 4 + zl) * WIDTH, WIDTH)
 
     z_on_up.wait_recv()
     z_on_down.wait_recv()
     crossed.append(cross(2, zblocks.at[turn(zh, 2)]))
     w3 = send_weight(3)
     w2_on = forward_weight(2, w2)
+    turn_weight(5, 6)
+    down_proj[...] = projection_t(down_seed_ref[0], col * HID, HID)
+    hidden_ranks = lax.dot_general(
+        down_proj[...], hidden[...], NT, preferred_element_type=jnp.float32
+    ) * (1.0 / math.sqrt(FF * 5461.25))
 
     pltpu.make_async_copy(grad_ref, grads.at[x, mine(y)], local_sem.at[3]).wait()
     for step in (1, 2, 3):
@@ -200,7 +204,7 @@
     def is_across(target):
         return lax.div(target, 2) != side
 
-    def part_copy(chunk, kind, target):
+    def part_copy(chunk, kind, target, source=None):
         if chunk == RANKS:
             at = ()
         else:
@@ -212,6 +216,8 @@
             sem = 2 + slot
         else:
             slot = 0 if kind == 0 else 1
+            if kind == 2 and chunk in DIRECT:
+                slot = 1 + lax.rem(zl, 2) if source is None else source
             dst = (rank_in if chunk == RANKS else part_in).at[(slot,) + at]
             sem = slot
         return pltpu.make_async_remote_copy(
@@ -222,7 +228,9 @@
 
     def wait_parts(chunk):
         part_copy(chunk, 0, mate).wait_recv()
-        part_copy(chunk, 2, lax.rem(zl + 2, 4)).wait_recv()
+        part_copy(chunk, 2, lax.rem(zl + 2, 4), 1).wait_recv()
+        if chunk in DIRECT:
+            part_copy(chunk, 2, lax.rem(zl + 2, 4), 2).wait_recv()
 
     def put(chunk, target, total):
         if chunk == RANKS:
@@ -252,7 +260,9 @@
                 product = jnp.dot(left, right, preferred_element_type=jnp.float32)
             total = product if part == 0 else total + product
 
-        keep = (target == zl) | (is_across(target) & inner)
+        keep = target == zl
+        if chunk not in DIRECT:
+            keep |= is_across(target) & inner
 
         @pl.when(keep)
         def _():
@@ -266,12 +276,21 @@
             put(chunk, target, total)
             part_copy(chunk, 0, target).start()
 
-        @pl.when(is_across(target) & jnp.logical_not(inner))
-        def _():
-            put(chunk, target, total)
-            part_copy(chunk, 1, target).start()
-
-        pending.append((chunk, target))
+        if chunk in DIRECT:
+
+            @pl.when(is_across(target))
+            def _():
+                put(chunk, target, total)
+                part_copy(chunk, 2, target).start()
+
+        else:
+
+            @pl.when(is_across(target) & jnp.logical_not(inner))
+            def _():
+                put(chunk, target, total)
+                part_copy(chunk, 1, target).start()
+
+            pending.append((chunk, target))
 
     def relay(most=0):
         while len(pending) > most:
@@ -302,7 +321,7 @@
         for lane in range(first, first + count):
             cols = slice(lane * 128, lane * 128 + 128)
             total = own[zl, :, cols]
-            for source in range(2):
+            for source in range(3 if chunk in DIRECT else 2):
                 total += part_in[source, lane].astype(jnp.float32)
             gate_out[:, cols] = (total * gate_factor[:, cols]).astype(jnp.bfloat16)
             up_out[:, cols] = (total * up_factor[:, cols]).astype(jnp.bfloat16)
@@ -442,9 +461,9 @@
     return pl.pallas_call(
         kernel,
         out_shape=(
-            jax.ShapeDtypeStruct((TOK, HID), bf16),
-            jax.ShapeDtypeStruct((TOK, HID), bf16),
-            jax.ShapeDtypeStruct((1, 2, RANK), f32),
+            pltpu.VMEM((TOK, HID), bf16),
+            pltpu.VMEM((TOK, HID), bf16),
+            pltpu.VMEM((1, 2, RANK), f32),
         ),
         in_specs=[hbm, hbm, hbm, hbm, smem, smem, smem],
         out_specs=(vmem, vmem, vmem),
@@ -463,7 +482,7 @@
             pltpu.VMEM((4, TOK, HID), f32),
             pltpu.VMEM((4, 7, TOK, 128), bf16),
             pltpu.VMEM((2, 7, TOK, 128), bf16),
-            pltpu.VMEM((2, 7, TOK, 128), bf16),
+            pltpu.VMEM((3, 7, TOK, 128), bf16),
             pltpu.VMEM((4, TOK, RANK), f32),
             pltpu.VMEM((4, TOK, RANK), bf16),
             pltpu.VMEM((2, TOK, RANK), bf16),

time: 85.3 us -> 82.7 us (0.970)
  Pallas kernels: 79.6 us -> 78 us
  local copies, waits for them, and re-layouts: 2.94 us -> 1.94 us
    pallas_call x1, Pallas kernels: 79.6 us -> 78 us  [shards(): pl.pallas_call(kernel, out_shape=(pltpu.VMEM((TOK, HID), bf16), pltpu.VME...]
    unnamed x7 -> x3, local copies, waits for them, and re-layouts: 2.94 us -> 1.94 us
where the time goes in v6:
time: 82.7 us; the launch traced here: 82.5 us
  Pallas kernels  78 us (94%)
  between operations  2.58 us (3%)
  local copies, waits for them, and re-layouts  1.94 us (2%)
    pallas_call x1, Pallas kernels, shards(): pl.pallas_call(kernel, out_shape=(pltpu.VMEM((TOK, HID), bf16), pltpu.VME...  78 us
    unnamed x3, local copies, waits for them, and re-layouts  1.94 us

profile of v6, /device:TPU:1, one launch (start us, length us, event | category | flops | bytes accessed | tf_op | source)
XLA Modules:
  0.0 82.5 jit_solution(961654960768357)
XLA Ops:
  2.6 78.0 %shard_map.94 = (bf16[128,896]{1,0:T(8,128)(2,1)S(1)}, bf16[128,896]{1,0:T(8,128)(2,1)S(1)}, f32[1,2,64]{2,1,0:T(2,128)S(1)}) custom-call(bf16[64,512]{1,0:T(8,128)(2,1)} %grad_ref.1, bf16[128,896]{1,0:T(8,128)(2,1)} %gate_ref.1, bf16[128,896]{1,0:T(8,128)(2,1)} %up_ref.1, bf16[896,512]{1,0:T(8,128)(2,1)} %weight_ref.1, s32[1]{0:T(128)S(6)} %copy.16.counts_ref, ...), custom_call_target="tpu_custom_call" | custom-call | tf_op jit(solution)/shard_map/pallas_call | solution.py:461
  80.6 0.7 copy.13
  81.3 0.6 copy.15
  81.8 0.7 copy.14

commit v7 on v6

--- a/solution.py
+++ b/solution.py
@@ -332,12 +332,12 @@
     across = [send(block, block, sibling)]
     w4 = send_weight(4)
     w3_on = forward_weight(3, w3)
+    w5 = send_weight(5)
 
     across[0].wait_recv()
     multiply(RANKS, turn(y, 0))
     wait_weights(w0_on, w1_on)
     multiply(0, turn(y, 0))
-    w5 = send_weight(5)
 
     relay()
     y_up.wait_recv()
@@ -350,11 +350,11 @@
     y_on_down = send(block, block, device(y=turn(y, 3)))
     block = y_block(turn(y, 1))
     across.append(send(block, block, sibling))
+    w6 = send_weight(6)
+    w4_on = forward_weight(4, w4)
     wait_weights(w2_on, w3_on)
     multiply(1, turn(y, 0))
     relay()
-    w4_on = forward_weight(4, w4)
-    w6 = send_weight(6)
 
     for place, step in ((1, 3), (2, 1)):
         across[place].wait_recv()

time: 82.7 us -> 82.6 us (level)
  no operation moved by 1% of the time
where the time goes in v7:
time: 82.6 us; the launch traced here: 82.5 us
  Pallas kernels  77.9 us (94%)
  between operations  2.58 us (3%)
  local copies, waits for them, and re-layouts  1.94 us (2%)
    pallas_call x1, Pallas kernels, shards(): pl.pallas_call(kernel, out_shape=(pltpu.VMEM((TOK, HID), bf16), pltpu.VME...  77.9 us
    unnamed x3, local copies, waits for them, and re-layouts  1.94 us

profile of v7, /device:TPU:1, one launch (start us, length us, event | category | flops | bytes accessed | tf_op | source)
XLA Modules:
  0.0 82.5 jit_solution(16481434703057199543)
XLA Ops:
  2.6 77.9 %shard_map.94 = (bf16[128,896]{1,0:T(8,128)(2,1)S(1)}, bf16[128,896]{1,0:T(8,128)(2,1)S(1)}, f32[1,2,64]{2,1,0:T(2,128)S(1)}) custom-call(bf16[64,512]{1,0:T(8,128)(2,1)} %grad_ref.1, bf16[128,896]{1,0:T(8,128)(2,1)} %gate_ref.1, bf16[128,896]{1,0:T(8,128)(2,1)} %up_ref.1, bf16[896,512]{1,0:T(8,128)(2,1)} %weight_ref.1, s32[1]{0:T(128)S(6)} %copy.16.counts_ref, ...), custom_call_target="tpu_custom_call" | custom-call | tf_op jit(solution)/shard_map/pallas_call | solution.py:461
  80.5 0.7 copy.13
  81.2 0.6 copy.15
  81.8 0.7 copy.14

commit v8 on v6

--- a/solution.py
+++ b/solution.py
@@ -327,9 +327,9 @@
             up_out[:, cols] = (total * up_factor[:, cols]).astype(jnp.bfloat16)
 
     block = y_block(y)
+    across = [send(block, block, sibling)]
     y_up = send(block, block, device(y=turn(y, 1)))
     y_down = send(block, block, device(y=turn(y, 3)))
-    across = [send(block, block, sibling)]
     w4 = send_weight(4)
     w3_on = forward_weight(3, w3)
 
@@ -341,15 +341,15 @@
 
     relay()
     y_up.wait_recv()
+    block = y_block(turn(y, 3))
+    across.append(send(block, block, sibling))
     block = y_block(turn(y, 3), 0, 2)
     y_on_up = send(block, block, device(y=turn(y, 1)))
-    block = y_block(turn(y, 3))
+    y_down.wait_recv()
+    block = y_block(turn(y, 1))
     across.append(send(block, block, sibling))
-    y_down.wait_recv()
     block = y_block(turn(y, 1), 2, 2)
     y_on_down = send(block, block, device(y=turn(y, 3)))
-    block = y_block(turn(y, 1))
-    across.append(send(block, block, sibling))
     wait_weights(w2_on, w3_on)
     multiply(1, turn(y, 0))
     relay()

time: 82.7 us -> 82.7 us (level)
  no operation moved by 1% of the time
where the time goes in v8:
time: 82.7 us; the launch traced here: 82.5 us
  Pallas kernels  78 us (94%)
  between operations  2.58 us (3%)
  local copies, waits for them, and re-layouts  1.94 us (2%)
    pallas_call x1, Pallas kernels, shards(): pl.pallas_call(kernel, out_shape=(pltpu.VMEM((TOK, HID), bf16), pltpu.VME...  78 us
    unnamed x3, local copies, waits for them, and re-layouts  1.94 us

profile of v8, /device:TPU:1, one launch (start us, length us, event | category | flops | bytes accessed | tf_op | source)
XLA Modules:
  0.0 82.5 jit_solution(2238676934866920620)
XLA Ops:
  2.6 78.0 %shard_map.94 = (bf16[128,896]{1,0:T(8,128)(2,1)S(1)}, bf16[128,896]{1,0:T(8,128)(2,1)S(1)}, f32[1,2,64]{2,1,0:T(2,128)S(1)}) custom-call(bf16[64,512]{1,0:T(8,128)(2,1)} %grad_ref.1, bf16[128,896]{1,0:T(8,128)(2,1)} %gate_ref.1, bf16[128,896]{1,0:T(8,128)(2,1)} %up_ref.1, bf16[896,512]{1,0:T(8,128)(2,1)} %weight_ref.1, s32[1]{0:T(128)S(6)} %copy.16.counts_ref, ...), custom_call_target="tpu_custom_call" | custom-call | tf_op jit(solution)/shard_map/pallas_call | solution.py:461
  80.6 0.7 copy.13
  81.3 0.6 copy.15
  81.8 0.7 copy.14

commit v9 on v6

--- a/solution.py
+++ b/solution.py
@@ -15,7 +15,7 @@
 WIDTH = 512
 HID = 896
 CHUNKS = ((0, 2), (2, 2), (4, 1), (5, 1), (6, 1))
-DIRECT = (3, 4)
+DIRECT = (4,)
 RANKS = len(CHUNKS)
 NT = (((1,), (1,)), ((), ()))
 MESH = pl.DeviceIdType.MESH

time: 82.7 us -> 83.6 us (1.011)
  Pallas kernels: 78 us -> 78.9 us
    pallas_call x1, Pallas kernels: 78 us -> 78.9 us  [shards(): pl.pallas_call(kernel, out_shape=(pltpu.VMEM((TOK, HID), bf16), pltpu.VME...]
where the time goes in v9:
time: 83.6 us; the launch traced here: 83.4 us
  Pallas kernels  78.9 us (94%)
  between operations  2.58 us (3%)
  local copies, waits for them, and re-layouts  1.94 us (2%)
    pallas_call x1, Pallas kernels, shards(): pl.pallas_call(kernel, out_shape=(pltpu.VMEM((TOK, HID), bf16), pltpu.VME...  78.9 us
    unnamed x3, local copies, waits for them, and re-layouts  1.94 us

profile of v9, /device:TPU:1, one launch (start us, length us, event | category | flops | bytes accessed | tf_op | source)
XLA Modules:
  0.0 83.4 jit_solution(2804475283498991816)
XLA Ops:
  2.6 78.9 %shard_map.94 = (bf16[128,896]{1,0:T(8,128)(2,1)S(1)}, bf16[128,896]{1,0:T(8,128)(2,1)S(1)}, f32[1,2,64]{2,1,0:T(2,128)S(1)}) custom-call(bf16[64,512]{1,0:T(8,128)(2,1)} %grad_ref.1, bf16[128,896]{1,0:T(8,128)(2,1)} %gate_ref.1, bf16[128,896]{1,0:T(8,128)(2,1)} %up_ref.1, bf16[896,512]{1,0:T(8,128)(2,1)} %weight_ref.1, s32[1]{0:T(128)S(6)} %copy.16.counts_ref, ...), custom_call_target="tpu_custom_call" | custom-call | tf_op jit(solution)/shard_map/pallas_call | solution.py:461
  81.5 0.7 copy.13
  82.2 0.6 copy.15
  82.7 0.7 copy.14

commit v10 on v6

--- a/solution.py
+++ b/solution.py
@@ -88,12 +88,10 @@
     for peer in peers:
         pl.semaphore_signal(barrier, inc=1, device_id=peer, device_id_type=MESH)
 
-    locals_[0].wait()
     def turn_weight(*pieces):
         for piece in pieces:
             weights[x, piece] = weight_in[piece * 128 : piece * 128 + 128, :].T
 
-    turn_weight(0, 1)
     pl.semaphore_wait(barrier, len(peers))
 
 
@@ -143,7 +141,10 @@
     z_up = send(grad_ref, zblocks.at[zh], device(zh=turn(zh, 1)))
     z_down = send(grad_ref, zblocks.at[zh], device(zh=turn(zh, 3)))
     crossed = [cross(0, grad_ref)]
+    locals_[0].wait()
+    turn_weight(0)
     w0 = send_weight(0)
+    turn_weight(1)
     w1 = send_weight(1)
 
     turn_weight(2)

time: 82.7 us -> 82.7 us (level)
  no operation moved by 1% of the time
where the time goes in v10:
time: 82.7 us; the launch traced here: 82.5 us
  Pallas kernels  78 us (94%)
  between operations  2.58 us (3%)
  local copies, waits for them, and re-layouts  1.94 us (2%)
    pallas_call x1, Pallas kernels, shards(): pl.pallas_call(kernel, out_shape=(pltpu.VMEM((TOK, HID), bf16), pltpu.VME...  78 us
    unnamed x3, local copies, waits for them, and re-layouts  1.94 us

profile of v10, /device:TPU:1, one launch (start us, length us, event | category | flops | bytes accessed | tf_op | source)
XLA Modules:
  0.0 82.5 jit_solution(16393815924803992715)
XLA Ops:
  2.6 78.0 %shard_map.94 = (bf16[128,896]{1,0:T(8,128)(2,1)S(1)}, bf16[128,896]{1,0:T(8,128)(2,1)S(1)}, f32[1,2,64]{2,1,0:T(2,128)S(1)}) custom-call(bf16[64,512]{1,0:T(8,128)(2,1)} %grad_ref.1, bf16[128,896]{1,0:T(8,128)(2,1)} %gate_ref.1, bf16[128,896]{1,0:T(8,128)(2,1)} %up_ref.1, bf16[896,512]{1,0:T(8,128)(2,1)} %weight_ref.1, s32[1]{0:T(128)S(6)} %copy.16.counts_ref, ...), custom_call_target="tpu_custom_call" | custom-call | tf_op jit(solution)/shard_map/pallas_call | solution.py:462
  80.6 0.7 copy.13
  81.3 0.6 copy.15
  81.8 0.7 copy.14
